TPU v7x, 128 devices: a whole 4x4x4 slice. The times are simulated.
128 devices in a mesh: row: 8 (over x, core), col: 16 (over y, z).
Axes of the slice: x: 4, y: 4, z: 4, core: 2. Of those that a mesh axis runs over, the one named last changes fastest.
Arguments:
- child_block: bfloat16 [8, 4096, 4096], P('row', None, 'col'), may hold values from -6 to 6
- left_gen: bfloat16 [8, 4096, 512], P('row', 'col'), may hold values from -0.25 to 0.25
- core_gen: bfloat16 [8, 512, 512], P('row'), may hold values from -0.25 to 0.25
- right_gen: bfloat16 [8, 512, 4096], P('row', None, 'col'), may hold values from -6 to 6
- child_maps: int32 [8, 4096], replicated, may hold values from 0 to 8191, as said below
- parent_entries: bfloat16 [8192, 8192], P('row', 'col'), may hold values from -6 to 6
- pivot_inverse: float32 [512, 512], replicated, may hold values from -0.01171875 to 0.01171875
Outputs:
- front: float32 [8192, 8192], P('row', 'col')
Inputs may be any that keep to these rules, and one draw needn't show every extreme that they name: `child_maps`: each row lists 4096 distinct parent indices. Within every aligned block of 256 positions of a row, at most 24 indices fall in any one of the 16 ranges of 512 consecutive parent indices, and some block of every row reaches it; within a whole row at most 768 fall in any one of the 8 ranges of 1024 consecutive parent indices, and every row reaches it in some range.
All inputs are finite; a program needn't handle non-finite values.
Results may differ from a plain program's by a relative error of at most 0.0047.
Values may be sent and summed in bfloat16 or wider, within the bound.
A program may use at most 128 MiB of HBM per device.

v0:
```python
import jax
import jax.numpy as jnp
from jax import lax
from jax.sharding import PartitionSpec as P


def broadcast(value, axis, source):
    kept = jnp.where(lax.axis_index(axis) == source, value, 0).astype(value.dtype)
    return lax.psum(kept, axis)


def row_layout(map_row, front_rows, row_count, row_slots):
    length = map_row.shape[0]
    group = map_row // front_rows
    onehot = (group[:, None] == jnp.arange(row_count, dtype=jnp.int32)[None, :]).astype(jnp.int32)
    ranks = jnp.sum((jnp.cumsum(onehot, axis=0) - 1) * onehot, axis=1)
    slot = group * row_slots + ranks
    total = row_count * row_slots
    source = jnp.full((total,), length, jnp.int32).at[slot].set(jnp.arange(length, dtype=jnp.int32))
    target = jnp.full((total,), front_rows, jnp.int32).at[slot].set(map_row - group * front_rows)
    return (source, target)


def col_layout(map_row, front_cols, col_count, col_slots):
    shard_pos = map_row.reshape(col_count, -1)
    width = shard_pos.shape[1]
    group = shard_pos // front_cols
    onehot = (group[:, :, None] == jnp.arange(col_count, dtype=jnp.int32)[None, None, :]).astype(
        jnp.int32
    )
    ranks = jnp.sum((jnp.cumsum(onehot, axis=1) - 1) * onehot, axis=2)
    slot = group * col_slots + ranks
    shard_ids = jnp.arange(col_count, dtype=jnp.int32)[:, None]
    positions = jnp.broadcast_to(jnp.arange(width, dtype=jnp.int32)[None, :], (col_count, width))
    total = col_count * col_slots
    source = jnp.full((col_count, total), width, jnp.int32).at[shard_ids, slot].set(positions)
    target = (
        jnp.full((col_count, total), front_cols, jnp.int32)
        .at[shard_ids, slot]
        .set(shard_pos - group * front_cols)
    )
    return (source, target)


def take_rows(matrix, lookup):
    padded = jnp.pad(matrix, ((0, 1), (0, 0)))
    return padded[lookup]


def take_both(matrix, row_lookup, col_lookup):
    rows_taken = take_rows(matrix, row_lookup)
    return take_rows(rows_taken.T, col_lookup).T


def inverse_map(targets, extent):
    count = targets.shape[0]
    filled = (
        jnp.full((extent + 1,), count, jnp.int32)
        .at[targets]
        .set(jnp.arange(count, dtype=jnp.int32))
    )
    return filled[:extent]


def on_device(
    child_block, left_gen, core_gen, right_gen, child_maps, parent_entries, pivot_inverse
):
    row_count = lax.axis_size("row")
    col_count = lax.axis_size("col")
    row_me = lax.axis_index("row")
    col_me = lax.axis_index("col")
    order_full = child_block.shape[1]
    front_rows, front_cols = parent_entries.shape
    unit_size = order_full // (16 * row_count * row_count)
    col_slots = 6 * unit_size
    row_slots = 12 * unit_size * col_count
    panel_width = pivot_inverse.shape[0]
    mixing = jnp.dot(core_gen[0], right_gen[0], preferred_element_type=jnp.float32).astype(
        jnp.bfloat16
    )
    own_block = child_block[0]
    product = jnp.dot(
        lax.all_gather(left_gen[0], "col", axis=0, tiled=True),
        mixing,
        preferred_element_type=jnp.float32,
    )
    update = (own_block.astype(jnp.float32) - product).astype(jnp.bfloat16)
    row_sources, row_targets = jax.vmap(
        lambda map_row: row_layout(map_row, front_rows, row_count, row_slots)
    )(child_maps)
    col_sources, col_targets = jax.vmap(
        lambda map_row: col_layout(map_row, front_cols, col_count, col_slots)
    )(child_maps)
    send_rows = row_sources[row_me]
    send_cols = col_sources[row_me][col_me]
    dest_rows = row_targets.reshape(row_count, row_count, row_slots)[:, row_me, :]
    dest_cols = col_targets.reshape(row_count, col_count, col_count, col_slots)[:, :, col_me, :]
    picked = take_both(update, send_rows, send_cols)
    assembled = parent_entries.astype(jnp.float32)
    slot_width = col_count * col_slots
    arranged = picked.reshape(row_count, row_slots, col_count, col_slots).transpose(0, 2, 1, 3)
    moved = lax.all_to_all(
        arranged.reshape(row_count * col_count, row_slots * col_slots),
        ("row", "col"),
        split_axis=0,
        concat_axis=0,
        tiled=True,
    )
    blocks = moved.reshape(row_count, col_count, row_slots, col_slots)

    def child_values(child):
        return blocks[child].transpose(1, 0, 2).reshape(row_slots, slot_width)

    def add_child(child, current):
        values = child_values(child)
        row_lookup = inverse_map(dest_rows[child], front_rows)
        col_lookup = inverse_map(dest_cols[child].reshape(slot_width), front_cols)
        placed = take_both(values, row_lookup, col_lookup)
        return current + placed.astype(jnp.float32)

    assembled = lax.fori_loop(0, row_count, add_child, assembled)
    local_panel = lax.cond(
        col_me == 0,
        lambda: jnp.dot(
            assembled,
            pivot_inverse,
            precision=lax.Precision.HIGHEST,
            preferred_element_type=jnp.float32,
        ),
        lambda: jnp.zeros((front_rows, panel_width), jnp.float32),
    )
    panel_rows = broadcast(local_panel, "col", 0)
    pivot = broadcast(assembled[:panel_width, :], "row", 0)
    trailing = assembled - jnp.dot(
        panel_rows, pivot, precision=lax.Precision.HIGHEST, preferred_element_type=jnp.float32
    )
    global_rows = row_me * front_rows + jnp.arange(front_rows, dtype=jnp.int32)
    global_cols = col_me * front_cols + jnp.arange(front_cols, dtype=jnp.int32)
    lower = jnp.where(global_cols[None, :] < panel_width, panel_rows, trailing)
    return jnp.where(global_rows[:, None] < panel_width, assembled, lower)


def solution(mesh):
    return jax.shard_map(
        on_device,
        mesh=mesh,
        in_specs=(
            P("row", None, "col"),
            P("row", "col", None),
            P("row", None, None),
            P("row", None, "col"),
            P(),
            P("row", "col"),
            P(),
        ),
        out_specs=P("row", "col"),
        check_vma=False,
    )
```

profile of v0, /device:TPU:0, one launch (start us, length us, event | category | flops | bytes accessed | tf_op | source)
XLA Modules:
  0.0 1292.8 jit_solution(9582393695233511523)
XLA Ops:
  9.9 125.2 %reduce-window.16 = s32[8,16,16,2,128]{4,2,3,1,0:T(8,128)S(1)} reduce-window(s32[8,16,16,2,128]{4,2,3,1,0:T(8,128)} %fusion.12, s32[]{:T(128)} %constant.181.clone.1), window={size=1x1x1x1x128 pad=0_0x0_0x0_0x0_0x127_0}, to_apply=%region_4.5 | reduce-window | flops 66584576 | bytes 4194308 | tf_op jit(solution)/shard_map/reduce-window.2
  142.8 120.2 %scatter_custom_fusion.3 = s32[49152]{0:T(1024)S(1)} fusion(s32[32768]{0:T(1024)S(1)} %bitcast.142, s32[32768]{0:T(1024)S(1)} %bitcast.146, s32[]{:T(128)} %constant.192.clone.1), kind=kCustom, calls=%fused_computation.102 | custom fusion | bytes 196612
  264.0 18.4 %reduce-window.14 = s32[8,8,32,128]{3,2,1,0:T(8,128)S(1)} reduce-window(s32[8,8,32,128]{3,2,1,0:T(8,128)S(1)} %fusion.14, s32[]{:T(128)} %constant.181.clone.1), window={size=1x1x1x128 pad=0_0x0_0x0_0x127_0}, to_apply=%region_0.1 | reduce-window | flops 33292288 | bytes 2097156 | tf_op jit(solution)/shard_map/reduce-window
  286.8 120.6 %scatter_custom_fusion.2 = s32[49152]{0:T(1024)S(1)} fusion(s32[32768]{0:T(1024)S(1)} %bitcast.144, s32[32768]{0:T(1024)S(1)} %bitcast.147, s32[]{:T(128)} %constant.183.clone.1), kind=kCustom, calls=%fused_computation.104 | custom fusion | bytes 196612
  422.4 24.9 %gather_fusion.2 = bf16[6144,256]{1,0:T(8,128)(2,1)} fusion(bf16[4097,256]{1,0:T(8,128)(2,1)S(1)} %pad.30.clone, s32[6144]{0:T(1024)S(1)} %broadcast_clamp_fusion), kind=kCustom, calls=%fused_computation.2 | custom fusion | bytes 6316032 | tf_op jit(solution)/shard_map/gather | solution.py:47
  454.3 5.5 gather_fusion.3
  459.8 5.9 copy.76
  465.8 21.5 %copy.56 = bf16[8,768,16,24]{3,1,2,0:T(8,128)(2,1)} copy(bf16[8,768,16,24]{1,0,3,2:T(8,128)(2,1)} %bitcast.131) | data formatting | bytes 9437184 | tf_op jit(solution)/shard_map/reshape | solution.py:101
  487.2 47.5 %all_to_all.8 = bf16[128,1,18432]{2,1,0:T(2,128)(2,1)} reshape(bf16[8,16,768,24]{3,2,1,0:T(8,128)(2,1)} %bitcast.128) | data formatting | bytes 9437184 | tf_op jit(solution)/shard_map/all_to_all | solution.py:102
  535.2 29.8 %reduce.21 = bf16[128,18432]{1,0:T(8,128)(2,1)} reduce(bf16[128,1,18432]{2,1,0:T(2,128)(2,1)} %all_to_all.8, bf16[]{:T(256)} %broadcast.485), dimensions={1}, to_apply=%all_to_all.8.reduce_sub_computation | reduce | bytes 9437186 | tf_op jit(solution)/shard_map/all_to_all | solution.py:102
  565.1 8.2 reshape.434
  573.2 11.6 all-to-all-start
  585.0 120.6 %scatter_custom_fusion.4 = s32[49152]{0:T(1024)S(1)} fusion(s32[32768]{0:T(1024)} %bitcast.145, s32[32768]{0:T(1024)S(1)} %bitcast.148, s32[]{:T(128)} %constant.179.clone.1), kind=kCustom, calls=%fused_computation.100 | custom fusion | bytes 197120
  706.3 120.4 %scatter_custom_fusion.5 = s32[49152]{0:T(1024)S(1)} fusion(s32[32768]{0:T(1024)} %bitcast.143, s32[32768]{0:T(1024)S(1)} %bitcast.149, s32[]{:T(128)} %constant.180.clone.1), kind=kCustom, calls=%fused_computation.98 | custom fusion | bytes 197120
  832.3 19.9 %reshape.435 = bf16[128,1,18432]{2,1,0:T(2,128)(2,1)} reshape(bf16[128,2,9216]{2,1,0:T(2,128)(2,1)} %all-to-all-done) | data formatting | bytes 9437184
  852.2 29.2 %reduce.12 = bf16[128,18432]{1,0:T(8,128)(2,1)} reduce(bf16[128,1,18432]{2,1,0:T(2,128)(2,1)} %reshape.435, bf16[]{:T(256)} %constant.248), dimensions={1}, to_apply=%all_to_all.7.reduce_sub_computation | reduce | bytes 9437186 | tf_op jit(solution)/shard_map/all_to_all | solution.py:102
  881.4 42.4 %reshape.320 = bf16[8,16,768,24]{3,2,1,0:T(8,128)(2,1)} reshape(bf16[128,18432]{1,0:T(8,128)(2,1)} %reduce.12) | data formatting | bytes 9437184 | tf_op jit(solution)/shard_map/reshape | solution.py:109
  923.8 21.6 %copy.59 = bf16[8,16,768,24]{2,3,1,0:T(8,128)(2,1)} copy(bf16[8,16,768,24]{3,2,1,0:T(8,128)(2,1)} %reshape.320) | data formatting | bytes 9437184 | tf_op jit(solution)/shard_map/while | solution.py:121
  945.4 174.8 %while.15 = (s32[]{:T(128)}, f32[1024,512]{0,1:T(8,128)S(1)}, bf16[8,16,768,24]{2,3,1,0:T(8,128)(2,1)}, s32[8,768]{1,0:T(8,128)}, s32[8,16,24]{2,1,0:T(8,128)S(1...) while((s32[]{:T(128)}, f32[1024,512]{0,1:T(8,128)S(1)}, bf16[8,16,768,24]{2,3,1,0:T(8,128)(2,1)}, ...), condition=%wide.region_13.14_spmd, body=%wide.region_10.13_spmd.sunk | while | flops 1058690 | bytes 15651197 | solution.py:121
  1121.5 6.2 conditional.1
  1121.7 6.0 fusion.43
  1132.7 52.2 %all-reduce.9.cloned.1.call-done = f32[512,512]{0,1:T(8,128)} async-done(((f32[512,512]{0,1:T(8,128)}), f32[512,512]{0,1:T(8,128)}) %all-reduce.9.cloned.1.call-update) | async-done | bytes 1048592 | tf_op jit(solution)/shard_map/psum | solution.py:9
  1184.9 93.1 %all-reduce.7.cloned.1.call-done = f32[1024,512]{1,0:T(8,128)} async-done(((f32[1024,512]{1,0:T(8,128)}), f32[1024,512]{1,0:T(8,128)}) %all-reduce.7.cloned.1.call-update) | async-done | bytes 2097168 | tf_op jit(solution)/shard_map/psum | solution.py:9
  1278.0 8.0 select_select_fusion
  (247 shorter events, 224.9 us)
Async XLA Ops:
  6.5 404.8 %copy-start = (bf16[1,512,512]{2,1,0:T(8,128)(2,1)S(1)}, bf16[1,512,512]{2,1,0:T(8,128)(2,1)}, u32[]{:S(2)}) copy-start(bf16[1,512,512]{2,1,0:T(8,128)(2,1)} %param.13) | copy-start | bytes 1572868
  6.5 404.8 %all-gather.3.cloned.1.call-start = ((), (), s32[]{:S(2)}) async-start(), calls=%async_computation.3 | async-start | bytes 4456448 | tf_op jit(solution)/shard_map/all_gather | solution.py:83
  137.1 4.0 copy-start.2
  140.9 1.3 copy-start.10
  141.0 1.3 copy-start.9
  142.7 120.3 %copy-start.5 = (s32[16,2,8,128]{3,1,2,0:T(2,128)}, s32[16,2,8,128]{3,1,2,0:T(2,128)S(1)}, u32[]{:S(2)}) copy-start(s32[16,2,8,128]{3,1,2,0:T(2,128)S(1)} %copy.74) | copy-start | bytes 393220
  285.7 0.7 copy-start.8
  285.7 0.8 copy-start.7
  286.8 120.7 %copy-start.6 = (s32[1,32,8,128]{3,1,2,0:T(8,128)}, s32[1,32,8,128]{3,1,2,0:T(8,128)S(1)}, u32[]{:S(2)}) copy-start(s32[1,32,8,128]{3,1,2,0:T(8,128)S(1)} %copy.71) | copy-start | bytes 393220
  407.5 3.8 copy-start.4
  573.2 259.1 %all-to-all-start = ((bf16[128,2,9216]{2,1,0:T(2,128)(2,1)}), bf16[128,2,9216]{2,1,0:T(2,128)(2,1)}, u32[]{:S(2)}, u32[]{:S(2)}) async-start(bf16[128,2,9216]{2,1,0:T(2,128)(2,1)} %reshape.434), calls=%async_computation | async-start | bytes 9437184 | tf_op jit(solution)/shard_map/all_to_all | solution.py:102
  584.9 243.6 %copy-start.3 = (bf16[1024,512]{1,0:T(8,128)(2,1)S(1)}, bf16[1024,512]{1,0:T(8,128)(2,1)}, u32[]{:S(2)}) copy-start(bf16[1024,512]{1,0:T(8,128)(2,1)} %param.16) | copy-start | bytes 3145732
  584.9 600.0 %all-reduce.9.cloned.1.call-start = ((), (), s32[]{:S(2)}) async-start(), calls=%async_computation.2 | async-start | bytes 2097152 | tf_op jit(solution)/shard_map/psum | solution.py:9
  1121.4 156.6 %all-reduce.7.cloned.1.call-start = ((), (), s32[]{:S(2)}) async-start(), calls=%async_computation.1 | async-start | bytes 4194304 | tf_op jit(solution)/shard_map/psum | solution.py:9
  1130.9 155.2 %copy-start.1 = (bf16[1,512,512]{2,1,0:T(8,128)(2,1)S(1)}, bf16[1,512,512]{2,1,0:T(8,128)(2,1)}, u32[]{:S(2)}) copy-start(bf16[1,512,512]{2,1,0:T(8,128)(2,1)} %param.13) | copy-start | bytes 1572868
Sparse Core Ops, SparseCore 0:
  9.5 54.2 all-gather.2
  1121.5 63.3 all-reduce.8
  1188.2 89.7 all-reduce.6
where the time goes:
time: 1310 us; the launch traced here: 1290 us
  local copies, waits for them, and re-layouts  863 us (66%)
  other arithmetic  238 us (18%)
  waiting for transfers between devices  146 us (11%)
  matrix products  19.2 us (1%)
  between operations  13.9 us (1%)
    unnamed x44, local copies, waits for them, and re-layouts  530 us
    another operation x4, other arithmetic  146 us
    psum x2, waiting for transfers between devices, broadcast(): return lax.psum(kept, axis)  145 us
    gather x18, local copies, waits for them, and re-layouts, take_rows(): return padded[lookup]  92.7 us
    all_to_all x2, other arithmetic, on_device(): lax.all_to_all(arranged.reshape(row_count * col_count, row_slots * col_sl...  59 us
    scatter x16, local copies, waits for them, and re-layouts, inverse_map(): filled = jnp.full((extent + 1,), count, jnp.int32).at[targets].set(jnp.ar...  50.5 us
    all_to_all x2, local copies, waits for them, and re-layouts, on_device(): lax.all_to_all(arranged.reshape(row_count * col_count, row_slots * col_sl...  48 us
    reshape x1, local copies, waits for them, and re-layouts, on_device(): blocks = moved.reshape(row_count, col_count, row_slots, col_slots)  42.4 us
  transfers between devices with their start and end apart: 4, of which 2 were waited for; matrix products, arithmetic and copies ran while one was open for 51% of the time, Pallas kernels for 0%

commit v1 on v0

v1 whole, which is shorter than its diff:
```python
import jax
import jax.numpy as jnp
from jax import lax
from jax.sharding import PartitionSpec as P

BF = jnp.bfloat16
F32 = jnp.float32
HI = lax.Precision.HIGHEST


def block_slots(mask, tri):
    ranks = jnp.dot(mask.astype(BF), tri, preferred_element_type=F32).astype(jnp.int32)
    return jnp.where(mask, ranks, -1)


def slot_targets(slots, targets, count):
    hit = slots[..., None, :] == jnp.arange(count, dtype=jnp.int32)[:, None]
    return jnp.sum(jnp.where(hit, targets[..., None, :] + 1, 0), axis=-1) - 1


def bcast(value, axis, source):
    kept = jnp.where(lax.axis_index(axis) == source, value, 0).astype(value.dtype)
    return lax.psum(kept, axis)


def on_device(
    child_block, left_gen, core_gen, right_gen, child_maps, parent_entries, pivot_inverse
):
    nr = lax.axis_size("row")
    nc = lax.axis_size("col")
    row_me = lax.axis_index("row")
    col_me = lax.axis_index("col")
    order = child_block.shape[1]
    width = child_block.shape[2]
    fr, fc = parent_entries.shape
    unit = order // (16 * nr * nr)
    cs = 6 * unit
    rs = 12 * unit
    pw = pivot_inverse.shape[0]
    nb = order // width

    left = lax.all_gather(left_gen[0], "col", axis=0, tiled=True)
    mixing = jnp.dot(core_gen[0], right_gen[0], preferred_element_type=F32).astype(BF)

    blocks = child_maps.reshape(nr, nb, width)
    pos = jnp.arange(width, dtype=jnp.int32)
    tri = (pos[:, None] < pos[None, :]).astype(BF)
    mine = lax.dynamic_index_in_dim(blocks, row_me, 0, keepdims=False)
    my_cols = lax.dynamic_index_in_dim(mine, col_me, 0, keepdims=False)
    cmask = (my_cols // fc)[None, :] == jnp.arange(nc, dtype=jnp.int32)[:, None]
    cslot = block_slots(cmask, tri)
    pick_cols = (cslot[:, None, :] == jnp.arange(cs, dtype=jnp.int32)[None, :, None]).astype(BF)
    pick_cols = pick_cols.reshape(nc * cs, width)
    rmask = (mine // fr)[:, None, :] == jnp.arange(nr, dtype=jnp.int32)[None, :, None]
    rslot = block_slots(rmask, tri)
    pick_rows = (rslot[:, :, None, :] == jnp.arange(rs, dtype=jnp.int32)[None, None, :, None]).astype(BF)
    pick_rows = pick_rows.reshape(nb, nr * rs, width)
    rmask2 = (blocks // fr) == row_me
    rtarget = slot_targets(block_slots(rmask2, tri), blocks - row_me * fr, rs).reshape(nr * nb * rs)
    place_rows = (rtarget[None, :] == jnp.arange(fr, dtype=jnp.int32)[:, None]).astype(BF)
    cmask2 = (blocks // fc) == col_me
    ctarget = slot_targets(block_slots(cmask2, tri), blocks - col_me * fc, cs).reshape(nr, nb * cs)
    place_cols = (ctarget[:, :, None] == jnp.arange(fc, dtype=jnp.int32)[None, None, :]).astype(BF)

    product = jnp.dot(left, mixing, preferred_element_type=F32)
    update = (child_block[0].astype(F32) - product).astype(BF)

    sent = lax.dot_general(pick_cols, update, (((1,), (1,)), ((), ())), preferred_element_type=F32)
    sent = sent.astype(BF).reshape(nc, cs, order)
    got = lax.all_to_all(sent, "col", split_axis=0, concat_axis=0, tiled=True)
    got = got.reshape(nc * cs, nb, width)
    rows = jnp.einsum("isp,cip->isc", pick_rows, got, preferred_element_type=F32).astype(BF)
    rows = rows.reshape(nb, nr, rs, nc * cs).transpose(1, 0, 2, 3)
    moved = lax.all_to_all(rows, "row", split_axis=0, concat_axis=0, tiled=True)
    moved = moved.reshape(nr, nb * rs, nc * cs)
    wide = jnp.einsum("nsc,ncf->nsf", moved, place_cols, preferred_element_type=F32).astype(BF)
    placed = jnp.dot(place_rows, wide.reshape(nr * nb * rs, fc), preferred_element_type=F32)
    assembled = parent_entries.astype(F32) + placed

    local_panel = lax.cond(
        col_me == 0,
        lambda: jnp.dot(assembled, pivot_inverse, precision=HI, preferred_element_type=F32),
        lambda: jnp.zeros((fr, pw), F32),
    )
    panel_rows = bcast(local_panel.astype(BF), "col", 0)
    pivot = bcast(assembled[:pw, :].astype(BF), "row", 0)
    trailing = assembled - jnp.dot(panel_rows, pivot, preferred_element_type=F32)
    global_rows = row_me * fr + jnp.arange(fr, dtype=jnp.int32)
    lower = jnp.where(col_me == 0, local_panel, trailing)
    return jnp.where(global_rows[:, None] < pw, assembled, lower)


def solution(mesh):
    return jax.shard_map(
        on_device,
        mesh=mesh,
        in_specs=(
            P("row", None, "col"),
            P("row", "col", None),
            P("row", None, None),
            P("row", None, "col"),
            P(),
            P("row", "col"),
            P(),
        ),
        out_specs=P("row", "col"),
        check_vma=False,
    )
```

time: 1310 us -> 361 us (0.28); the launches traced: 1290 us -> 361 us
  local copies, waits for them, and re-layouts: 863 us -> 9.84 us
  other arithmetic: 238 us -> 7.69 us
  waiting for transfers between devices: 146 us -> 287 us
    unnamed x44 -> x11, local copies, waits for them, and re-layouts: 530 us -> 6.8 us
    another operation x4 -> x0, other arithmetic: 146 us -> none
    gather x18 -> x0, local copies, waits for them, and re-layouts: 92.7 us -> none  [take_rows(): return padded[lookup]]
    all_to_all x1 -> x2, waiting for transfers between devices: 0.01 us -> 91 us  [the longest x1 49.8 us: on_device(): moved = lax.all_to_all(rows, 'row', split_axis=0, concat_axis=0, tiled=True)]
    reshape x12 -> x1, local copies, waits for them, and re-layouts: 68 us -> 2.68 us  [on_device(): rows = rows.reshape(nb, nr, rs, nc * cs).transpose(1, 0, 2, 3)]
    all_to_all x2 -> x0, other arithmetic: 59 us -> none  [on_device(): lax.all_to_all(arranged.reshape(row_count * col_count, row_slots * col_sl...]
    all_gather x1, waiting for transfers between devices: 0.02 us -> 51.8 us  [on_device(): left = lax.all_gather(left_gen[0], 'col', axis=0, tiled=True)]
    scatter x18 -> x0, local copies, waits for them, and re-layouts: 51.2 us -> none  [the longest x16 50.5 us: inverse_map(): filled = jnp.full((extent + 1,), count, jnp.int32).at[targets].set(jnp.ar...]
  transfers between devices with their start and end apart: 4 -> 5, of which waited for: 2 -> 5; matrix products, arithmetic and copies ran while one was open for 51% -> 5% of each run, Pallas kernels for 0% -> 0%
where the time goes in v1:
time: 361 us
  waiting for transfers between devices  287 us (80%)
  matrix products  32.1 us (9%)
  between operations  13.3 us (4%)
  starting transfers between devices  10.3 us (3%)
  local copies, waits for them, and re-layouts  9.84 us (3%)
  other arithmetic  7.69 us (2%)
    psum x2, waiting for transfers between devices, bcast(): return lax.psum(kept, axis)  144 us
    all_gather x1, waiting for transfers between devices, on_device(): left = lax.all_gather(left_gen[0], 'col', axis=0, tiled=True)  51.8 us
    all_to_all x1, waiting for transfers between devices, on_device(): moved = lax.all_to_all(rows, 'row', split_axis=0, concat_axis=0, tiled=True)  49.8 us
    all_to_all x1, waiting for transfers between devices, on_device(): got = lax.all_to_all(sent, 'col', split_axis=0, concat_axis=0, tiled=True)  41.2 us
  transfers between devices with their start and end apart: 5, of which 5 were waited for; matrix products, arithmetic and copies ran while one was open for 5% of the time, Pallas kernels for 0%

profile of v1, /device:TPU:0, one launch (start us, length us, event | category | flops | bytes accessed | tf_op | source)
XLA Modules:
  0.0 360.6 jit_solution(2756024005519553071)
XLA Ops:
  6.5 0.7 all-gather.3.cloned.1.call-update
  7.3 1.0 copy.43
  8.3 2.9 copy.15
  11.9 51.8 %all-gather.3.cloned.1.call-done = bf16[1,4096,512]{2,1,0:T(8,128)(2,1)} async-done(((bf16[1,256,512]{2,1,0:T(8,128)(2,1)}), bf16[1,4096,512]{2,1,0:T(8,128)(2,1)}) %all-gather.3.cloned.1.call-update) | async-done | bytes 4194320 | tf_op jit(solution)/shard_map/all_gather | solution.py:42
  63.7 6.0 %convolution_convert_fusion = bf16[384,4096]{1,0:T(8,128)(2,1)} fusion(pred[384,256]{1,0:T(32,128)(4,1)S(1)} %bitcast_compare_fusion.1, bf16[512,256]{1,0:T(8,128)(2,1)S(1)} %convolution_convert_fusion.1, bf16[1,4096,512]{2,1,0:T(8,128)(2,1)} %all-gather.3.cloned.1.call-done, bf16[1,4096,256]{1,2,0:T(8,128)(2,1)S(1)} %copy.15), kind=kOutput, calls=%fused_computation.8 | convolution fusion | flops 1883766784 | bytes 9797632 | tf_op jit(solution)/shard_map/dot_general | solution.py:68
  69.6 5.3 %all-to-all-start = ((bf16[16,24,4096]{2,1,0:T(8,128)(2,1)}), bf16[16,24,4096]{2,1,0:T(8,128)(2,1)}, u32[]{:S(2)}, u32[]{:S(2)}) async-start(bf16[16,24,4096]{2,1,0:T(8,128)(2,1)} %bitcast.92), calls=%async_computation | async-start | bytes 6291456 | tf_op jit(solution)/shard_map/all_to_all | solution.py:70
  75.3 1.0 bitcast_compare_fusion
  76.3 41.2 %all-to-all-done = bf16[16,24,4096]{2,1,0:T(8,128)(2,1)} async-done(((bf16[16,24,4096]{2,1,0:T(8,128)(2,1)}), bf16[16,24,4096]{2,1,0:T(8,128)(2,1)}, u32[]{:S(2)}, u32[]{:S(2)}) %all-to-all-start) | async-done | bytes 3145760 | tf_op jit(solution)/shard_map/all_to_all | solution.py:70
  117.5 2.9 copy.19
  120.4 2.6 fusion.10
  123.0 2.7 copy.42
  125.7 4.7 %all-to-all-start.1 = ((bf16[8,16,48,384]{3,2,1,0:T(8,128)(2,1)}), bf16[8,16,48,384]{3,2,1,0:T(8,128)(2,1)}, u32[]{:S(2)}, u32[]{:S(2)}) async-start(bf16[8,16,48,384]{3,2,1,0:T(8,128)(2,1)} %bitcast.89), calls=%async_computation.1 | async-start | bytes 9437184 | tf_op jit(solution)/shard_map/all_to_all | solution.py:74
  131.0 2.2 select_reduce_fusion.1
  133.6 2.2 select_reduce_fusion
  136.0 49.8 %all-to-all-done.1 = bf16[8,16,48,384]{3,2,1,0:T(8,128)(2,1)} async-done(((bf16[8,16,48,384]{3,2,1,0:T(8,128)(2,1)}), bf16[8,16,48,384]{3,2,1,0:T(8,128)(2,1)}, u32[]{:S(2)}, u32[]{:S(2)}) %all-to-all-start.1) | async-done | bytes 4718624 | tf_op jit(solution)/shard_map/all_to_all | solution.py:74
  185.7 5.6 %fusion.6 = bf16[8,768,512]{2,1,0:T(8,128)(2,1)S(1)} fusion(bf16[8,768,384]{2,1,0:T(8,128)(2,1)} %bitcast.13, s32[8,384]{1,0:T(8,128)S(1)} %sub.72), kind=kOutput, calls=%fused_computation.14 | convolution fusion | flops 2420637696 | bytes 11022336 | tf_op jit(solution)/shard_map/nsc,ncf->nsf/dot_general | solution.py:76
  191.4 6.7 %convert_add_fusion = f32[1024,512]{1,0:T(8,128)S(1)} fusion(bf16[1024,512]{1,0:T(8,128)(2,1)S(1)} %copy-done.3, bf16[6144,512]{1,0:T(8,128)(2,1)S(1)} %bitcast.100, s32[6144]{0:T(1024)S(1)} %sub.64), kind=kOutput, calls=%fused_computation.22 | convolution fusion | flops 6449790976 | bytes 9461760 | tf_op jit(solution)/shard_map/dot_general | solution.py:77
  198.1 0.9 fusion.19
  199.0 6.0 %conditional.1 = (f32[1024,512]{1,0:T(8,128)}, bf16[1024,512]{1,0:T(8,128)(2,1)S(1)}) conditional(s32[]{:T(128)} %convert_element_type.71, () %tuple.15, (f32[1024,512]{1,0:T(8,128)S(1)}, f32[512,512]{1,0:T(8,128)}) %tuple.16), branch_computations={%region_2.3_spmd, %region_3.4_spmd} | conditional | flops 3221749760 | bytes 6291472 | solution.py:80
  199.0 6.0 %fusion.63 = (bf16[1024,512]{1,0:T(8,128)(2,1)S(1)}, f32[1024,512]{1,0:T(8,128)}) fusion(f32[1024,512]{1,0:T(8,128)S(1)} %get-tuple-element.11, f32[512,512]{1,0:T(8,128)} %get-tuple-element.18), kind=kOutput, calls=%fused_computation.100 | convolution fusion | flops 3221749760 | bytes 6291456 | tf_op jit(solution)/shard_map/cond/branch_1_fun/dot_general | solution.py:82
  205.0 1.1 broadcast_select_fusion
  206.1 53.8 %all-reduce.5.cloned.1.call-done = bf16[512,512]{1,0:T(8,128)(2,1)} async-done(((bf16[512,512]{1,0:T(8,128)(2,1)}), bf16[512,512]{1,0:T(8,128)(2,1)}) %all-reduce.5.cloned.1.call-update) | async-done | bytes 524304 | tf_op jit(solution)/shard_map/psum | solution.py:23
  260.0 90.0 %all-reduce.3.cloned.1.call-done = bf16[1024,512]{1,0:T(8,128)(2,1)} async-done(((bf16[1024,512]{1,0:T(8,128)(2,1)}), bf16[1024,512]{1,0:T(8,128)(2,1)}) %all-reduce.3.cloned.1.call-update) | async-done | bytes 1048592 | tf_op jit(solution)/shard_map/psum | solution.py:23
  350.0 4.1 %select_select_fusion = f32[1024,512]{1,0:T(8,128)} fusion(f32[1024,512]{1,0:T(8,128)S(1)} %convert_add_fusion, f32[1024,512]{1,0:T(8,128)} %get-tuple-element.15, bf16[1024,512]{1,0:T(8,128)(2,1)} %all-reduce.3.cloned.1.call-done, bf16[512,512]{1,0:T(8,128)(2,1)} %all-reduce.5.cloned.1.call-done, pred[1024]{0:T(1024)(128)(4,1)S(1)} %add_compare_fusion, ...), kind=kOutput, calls=%fused_computation.21 | convolution fusion | flops 538443776 | bytes 7865345 | tf_op jit(solution)/shard_map/dot_general | solution.py:87
  (32 shorter events, 2.0 us)
Async XLA Ops:
  6.5 5.0 %copy-start = (bf16[1,512,512]{2,1,0:T(8,128)(2,1)S(1)}, bf16[1,512,512]{2,1,0:T(8,128)(2,1)}, u32[]{:S(2)}) copy-start(bf16[1,512,512]{2,1,0:T(8,128)(2,1)} %param.11) | copy-start | bytes 1572868
  6.5 5.1 %copy-start.2 = (bf16[1,512,256]{2,1,0:T(8,128)(2,1)S(1)}, bf16[1,512,256]{2,1,0:T(8,128)(2,1)}, u32[]{:S(2)}) copy-start(bf16[1,512,256]{2,1,0:T(8,128)(2,1)} %param.12) | copy-start | bytes 786436
  6.5 57.1 %all-gather.3.cloned.1.call-start = ((), (), s32[]{:S(2)}) async-start(), calls=%async_computation.4 | async-start | bytes 4456448 | tf_op jit(solution)/shard_map/all_gather | solution.py:42
  69.6 47.9 %all-to-all-start = ((bf16[16,24,4096]{2,1,0:T(8,128)(2,1)}), bf16[16,24,4096]{2,1,0:T(8,128)(2,1)}, u32[]{:S(2)}, u32[]{:S(2)}) async-start(bf16[16,24,4096]{2,1,0:T(8,128)(2,1)} %bitcast.92), calls=%async_computation | async-start | bytes 6291456 | tf_op jit(solution)/shard_map/all_to_all | solution.py:70
  125.7 5.0 %copy-start.1 = (s32[8,4096]{1,0:T(8,128)S(1)}, s32[8,4096]{1,0:T(8,128)}, u32[]{:S(2)}) copy-start(s32[8,4096]{1,0:T(8,128)} %param.13) | copy-start | bytes 393220
  125.7 60.0 %all-to-all-start.1 = ((bf16[8,16,48,384]{3,2,1,0:T(8,128)(2,1)}), bf16[8,16,48,384]{3,2,1,0:T(8,128)(2,1)}, u32[]{:S(2)}, u32[]{:S(2)}) async-start(bf16[8,16,48,384]{3,2,1,0:T(8,128)(2,1)} %bitcast.89), calls=%async_computation.1 | async-start | bytes 9437184 | tf_op jit(solution)/shard_map/all_to_all | solution.py:74
  130.4 129.5 %all-reduce.5.cloned.1.call-start = ((), (), s32[]{:S(2)}) async-start(), calls=%async_computation.3 | async-start | bytes 1048576 | tf_op jit(solution)/shard_map/psum | solution.py:23
  185.7 5.7 %copy-start.3 = (bf16[1024,512]{1,0:T(8,128)(2,1)S(1)}, bf16[1024,512]{1,0:T(8,128)(2,1)}, u32[]{:S(2)}) copy-start(bf16[1024,512]{1,0:T(8,128)(2,1)} %param.14) | copy-start | bytes 3145732
  198.9 151.1 %all-reduce.3.cloned.1.call-start = ((), (), s32[]{:S(2)}) async-start(), calls=%async_computation.2 | async-start | bytes 2097152 | tf_op jit(solution)/shard_map/psum | solution.py:23
Sparse Core Ops, SparseCore 0:
  9.5 54.1 all-gather.2
  199.1 60.8 all-reduce.4
  263.6 86.3 all-reduce.2

commit v2 on v1

--- a/solution.py
+++ b/solution.py
@@ -1,6 +1,8 @@
 import jax
 import jax.numpy as jnp
 from jax import lax
+from jax.experimental import pallas as pl
+from jax.experimental.pallas import tpu as pltpu
 from jax.sharding import PartitionSpec as P
 
 BF = jnp.bfloat16
@@ -18,9 +20,142 @@
     return jnp.sum(jnp.where(hit, targets[..., None, :] + 1, 0), axis=-1) - 1
 
 
-def bcast(value, axis, source):
-    kept = jnp.where(lax.axis_index(axis) == source, value, 0).astype(value.dtype)
-    return lax.psum(kept, axis)
+def col_peer(me, d):
+    y = lax.rem(me // 4 + d // 4, 4)
+    z = lax.rem(lax.rem(me, 4) + lax.rem(d, 4), 4)
+    return y * 4 + z
+
+
+def row_peer(me, d):
+    x = lax.rem(me // 2 + d // 2, 4)
+    core = lax.rem(lax.rem(me, 2) + lax.rem(d, 2), 2)
+    return x * 2 + core
+
+
+def col_from(me, d):
+    y = lax.rem(me // 4 + 4 - d // 4, 4)
+    z = lax.rem(lax.rem(me, 4) + 4 - lax.rem(d, 4), 4)
+    return y * 4 + z
+
+
+def row_from(me, d):
+    x = lax.rem(me // 2 + 4 - d // 2, 4)
+    core = lax.rem(lax.rem(me, 2) + lax.rem(d, 2), 2)
+    return x * 2 + core
+
+
+def each(low, high, body):
+    def step(i, carry):
+        body(i)
+        return carry
+
+    lax.fori_loop(low, high, step, 0)
+
+
+def greet(nr, nc, row, col):
+    barrier = pltpu.get_barrier_semaphore()
+    each(1, nc, lambda d: pl.semaphore_signal(
+        barrier, inc=1, device_id={"col": col_peer(col, d)}, device_id_type=pl.DeviceIdType.MESH))
+    each(1, nr, lambda d: pl.semaphore_signal(
+        barrier, inc=1, device_id={"row": row_peer(row, d)}, device_id_type=pl.DeviceIdType.MESH))
+    pl.semaphore_wait(barrier, nc + nr - 2)
+
+
+def share_kernel(nr, nc, asm, pinv, panel, pivot, chunk, ss1, rs1, ss2, rs2, ss3, rs3, ss4, rs4):
+    row = lax.axis_index("row")
+    col = lax.axis_index("col")
+    mesh = pl.DeviceIdType.MESH
+    pc = panel.shape[0] // nc
+    vc = pivot.shape[0] // nr
+
+    def rows_of(ref, index, size):
+        return ref.at[pl.ds(pl.multiple_of(index * size, size), size)]
+
+    def pivot_out(d):
+        return pltpu.make_async_remote_copy(
+            rows_of(asm, d, vc), rows_of(pivot, d, vc), ss1.at[d], rs1.at[0],
+            device_id={"row": d}, device_id_type=mesh)
+
+    def panel_out(d):
+        return pltpu.make_async_remote_copy(
+            rows_of(asm, d, pc), chunk, ss2.at[d], rs2.at[0],
+            device_id={"col": d}, device_id_type=mesh)
+
+    def pivot_share(d, whose):
+        part = rows_of(pivot, whose, vc)
+        return pltpu.make_async_remote_copy(
+            part, part, ss3.at[d], rs3.at[d],
+            device_id={"row": row_peer(row, d)}, device_id_type=mesh)
+
+    def panel_share(d, whose):
+        part = rows_of(panel, whose, pc)
+        return pltpu.make_async_remote_copy(
+            part, part, ss4.at[d], rs4.at[d],
+            device_id={"col": col_peer(col, d)}, device_id_type=mesh)
+
+    greet(nr, nc, row, col)
+
+    @pl.when(col == 0)
+    def _():
+        each(1, nc, lambda d: panel_out(d).start())
+        chunk[...] = asm[0:pc, :]
+
+    @pl.when(row == 0)
+    def _():
+        each(1, nr, lambda d: pivot_out(d).start())
+        pivot[0:vc, :] = asm[0:vc, :]
+
+    @pl.when(row > 0)
+    def _():
+        pivot_out(row).wait_recv()
+
+    each(1, nr, lambda d: pivot_share(d, row).start())
+
+    @pl.when(col > 0)
+    def _():
+        panel_out(col).wait_recv()
+
+    part = jnp.dot(chunk[...].astype(F32), pinv[...], precision=HI, preferred_element_type=F32)
+    panel[pl.ds(pl.multiple_of(col * pc, pc), pc), :] = part.astype(BF)
+    each(1, nc, lambda d: panel_share(d, col).start())
+
+    each(1, nr, lambda d: pivot_share(d, row_from(row, d)).wait_recv())
+    each(1, nc, lambda d: panel_share(d, col_from(col, d)).wait_recv())
+    each(1, nr, lambda d: pivot_share(d, row).wait_send())
+    each(1, nc, lambda d: panel_share(d, col).wait_send())
+
+    @pl.when(col == 0)
+    def _():
+        each(1, nc, lambda d: panel_out(d).wait_send())
+
+    @pl.when(row == 0)
+    def _():
+        each(1, nr, lambda d: pivot_out(d).wait_send())
+
+
+def share(nr, nc, asm, pinv):
+    rows, cols = asm.shape
+    vmem = pl.BlockSpec(memory_space=pltpu.VMEM)
+    dma = pltpu.SemaphoreType.DMA
+    pw = pinv.shape[0]
+    return pl.pallas_call(
+        lambda *refs: share_kernel(nr, nc, *refs),
+        out_shape=(
+            jax.ShapeDtypeStruct((rows, pw), BF),
+            jax.ShapeDtypeStruct((pw, cols), BF),
+        ),
+        in_specs=[vmem, vmem],
+        out_specs=(vmem, vmem),
+        scratch_shapes=[
+            pltpu.VMEM((rows // nc, pw), BF),
+            dma((nr,)), dma((1,)), dma((nc,)), dma((1,)),
+            dma((nr,)), dma((nr,)), dma((nc,)), dma((nc,)),
+        ],
+        compiler_params=pltpu.CompilerParams(
+            collective_id=0, has_side_effects=True, vmem_limit_bytes=32 * 1024 * 1024
+        ),
+        name="share",
+    )(asm, pinv)
 
 
 def on_device(
@@ -77,13 +212,12 @@
     placed = jnp.dot(place_rows, wide.reshape(nr * nb * rs, fc), preferred_element_type=F32)
     assembled = parent_entries.astype(F32) + placed
 
+    panel_rows, pivot = share(nr, nc, assembled.astype(BF), pivot_inverse)
     local_panel = lax.cond(
         col_me == 0,
         lambda: jnp.dot(assembled, pivot_inverse, precision=HI, preferred_element_type=F32),
         lambda: jnp.zeros((fr, pw), F32),
     )
-    panel_rows = bcast(local_panel.astype(BF), "col", 0)
-    pivot = bcast(assembled[:pw, :].astype(BF), "row", 0)
     trailing = assembled - jnp.dot(panel_rows, pivot, preferred_element_type=F32)
     global_rows = row_me * fr + jnp.arange(fr, dtype=jnp.int32)
     lower = jnp.where(col_me == 0, local_panel, trailing)

time: 361 us -> 253 us (0.70)
  waiting for transfers between devices: 287 us -> 143 us
  Pallas kernels: 0 us -> 35.8 us
    psum x2 -> x0, waiting for transfers between devices: 144 us -> none  [bcast(): return lax.psum(kept, axis)]
    pallas_call x0 -> x1, Pallas kernels: none -> 35.8 us  [share(): pl.pallas_call(lambda *refs: share_kernel(nr, nc, *refs), out_shape=(jax....]
  transfers between devices with their start and end apart: 5 -> 3, of which waited for: 5 -> 3; matrix products, arithmetic and copies ran while one was open for 5% -> 4% of each run, Pallas kernels for 0% -> 0%
where the time goes in v2:
time: 253 us
  waiting for transfers between devices  143 us (57%)
  Pallas kernels  35.8 us (14%)
  matrix products  34.2 us (14%)
  between operations  13.6 us (5%)
  starting transfers between devices  10.2 us (4%)
  local copies, waits for them, and re-layouts  9.86 us (4%)
  other arithmetic  5.74 us (2%)
    all_gather x1, waiting for transfers between devices, on_device(): left = lax.all_gather(left_gen[0], 'col', axis=0, tiled=True)  51.8 us
    all_to_all x1, waiting for transfers between devices, on_device(): moved = lax.all_to_all(rows, 'row', split_axis=0, concat_axis=0, tiled=True)  49.8 us
    all_to_all x1, waiting for transfers between devices, on_device(): got = lax.all_to_all(sent, 'col', split_axis=0, concat_axis=0, tiled=True)  41.2 us
    pallas_call x1, Pallas kernels, share(): pl.pallas_call(lambda *refs: share_kernel(nr, nc, *refs), out_shape=(jax....  35.8 us
    dot_general x1, matrix products, on_device(): jnp.dot(place_rows, wide.reshape(nr * nb * rs, fc), preferred_element_typ...  8 us
    unnamed x13, local copies, waits for them, and re-layouts  6.81 us
    dot_general x1, matrix products, on_device(): jnp.dot(assembled, pivot_inverse, precision=HI, preferred_element_type=F32)  6.36 us
    dot_general x1, matrix products, on_device(): lax.dot_general(pick_cols, update, (((1,), (1,)), ((), ())), preferred_el...  5.99 us
  transfers between devices with their start and end apart: 3, of which 3 were waited for; matrix products, arithmetic and copies ran while one was open for 4% of the time, Pallas kernels for 0%

profile of v2, /device:TPU:0, one launch (start us, length us, event | category | flops | bytes accessed | tf_op | source)
XLA Modules:
  0.0 252.9 jit_solution(716571291755900346)
XLA Ops:
  6.5 0.7 all-gather.3.cloned.1.call-update
  7.3 1.0 copy.42
  8.3 2.9 %copy.14 = bf16[1,4096,256]{1,2,0:T(8,128)(2,1)S(1)} copy(bf16[1,4096,256]{2,1,0:T(8,128)(2,1)} %param.9) | data formatting | bytes 4194304 | tf_op args[0]
  11.6 0.3 convolution_convert_fusion.1
  11.9 51.8 %all-gather.3.cloned.1.call-done = bf16[1,4096,512]{2,1,0:T(8,128)(2,1)} async-done(((bf16[1,256,512]{2,1,0:T(8,128)(2,1)}), bf16[1,4096,512]{2,1,0:T(8,128)(2,1)}) %all-gather.3.cloned.1.call-update) | async-done | bytes 4194320 | tf_op jit(solution)/shard_map/all_gather | solution.py:177
  63.7 6.0 %convolution_convert_fusion = bf16[384,4096]{1,0:T(8,128)(2,1)} fusion(pred[384,256]{1,0:T(32,128)(4,1)S(1)} %bitcast_compare_fusion.1, bf16[512,256]{1,0:T(8,128)(2,1)S(1)} %convolution_convert_fusion.1, bf16[1,4096,512]{2,1,0:T(8,128)(2,1)} %all-gather.3.cloned.1.call-done, bf16[1,4096,256]{1,2,0:T(8,128)(2,1)S(1)} %copy.14), kind=kOutput, calls=%fused_computation.8 | convolution fusion | flops 1883766784 | bytes 9797632 | tf_op jit(solution)/shard_map/dot_general | solution.py:203
  69.7 5.3 %all-to-all-start = ((bf16[16,24,4096]{2,1,0:T(8,128)(2,1)}), bf16[16,24,4096]{2,1,0:T(8,128)(2,1)}, u32[]{:S(2)}, u32[]{:S(2)}) async-start(bf16[16,24,4096]{2,1,0:T(8,128)(2,1)} %bitcast.92), calls=%async_computation | async-start | bytes 6291456 | tf_op jit(solution)/shard_map/all_to_all | solution.py:205
  75.3 1.0 bitcast_compare_fusion
  76.3 41.2 %all-to-all-done = bf16[16,24,4096]{2,1,0:T(8,128)(2,1)} async-done(((bf16[16,24,4096]{2,1,0:T(8,128)(2,1)}), bf16[16,24,4096]{2,1,0:T(8,128)(2,1)}, u32[]{:S(2)}, u32[]{:S(2)}) %all-to-all-start) | async-done | bytes 3145760 | tf_op jit(solution)/shard_map/all_to_all | solution.py:205
  117.5 2.9 %copy.18 = bf16[48,8,16,256]{3,2,1,0:T(8,128)(2,1)S(1)} copy(bf16[48,8,16,256]{3,1,2,0:T(8,128)(2,1)} %bitcast.19) | data formatting | bytes 6291456
  120.4 2.6 %fusion.10 = bf16[16,384,384]{2,1,0:T(8,128)(2,1)S(1)} fusion(pred[16,384,256]{2,1,0:T(32,128)(4,1)S(1)} %bitcast_compare_fusion, bf16[384,16,256]{2,1,0:T(8,128)(2,1)S(1)} %bitcast.91), kind=kOutput, calls=%fused_computation.20 | convolution fusion | flops 1210318848 | bytes 9437184 | tf_op jit(solution)/shard_map/isp,cip->isc/dot_general | solution.py:207
  123.0 2.7 %copy.41 = bf16[16,8,48,384]{3,2,0,1:T(8,128)(2,1)} copy(bf16[16,8,48,384]{3,2,1,0:T(8,128)(2,1)S(1)} %bitcast.90) | data formatting | bytes 9437184 | tf_op jit(solution)/shard_map/reshape | solution.py:208
  125.7 4.9 %all-to-all-start.1 = ((bf16[8,16,48,384]{3,2,1,0:T(8,128)(2,1)}), bf16[8,16,48,384]{3,2,1,0:T(8,128)(2,1)}, u32[]{:S(2)}, u32[]{:S(2)}) async-start(bf16[8,16,48,384]{3,2,1,0:T(8,128)(2,1)} %bitcast.89), calls=%async_computation.1 | async-start | bytes 9437184 | tf_op jit(solution)/shard_map/all_to_all | solution.py:209
  130.6 0.2 fusion.15
  131.0 2.2 select_reduce_fusion.1
  133.3 0.2 fusion.17
  133.6 2.2 select_reduce_fusion
  135.9 49.8 %all-to-all-done.1 = bf16[8,16,48,384]{3,2,1,0:T(8,128)(2,1)} async-done(((bf16[8,16,48,384]{3,2,1,0:T(8,128)(2,1)}), bf16[8,16,48,384]{3,2,1,0:T(8,128)(2,1)}, u32[]{:S(2)}, u32[]{:S(2)}) %all-to-all-start.1) | async-done | bytes 4718624 | tf_op jit(solution)/shard_map/all_to_all | solution.py:209
  185.7 5.9 %fusion.6 = bf16[8,768,512]{2,1,0:T(8,128)(2,1)S(1)} fusion(bf16[8,768,384]{2,1,0:T(8,128)(2,1)} %bitcast.13, s32[8,384]{1,0:T(8,128)S(1)} %sub.72), kind=kOutput, calls=%fused_computation.14 | convolution fusion | flops 2420637696 | bytes 11022336 | tf_op jit(solution)/shard_map/nsc,ncf->nsf/dot_general | solution.py:211
  191.6 8.0 %fusion.62 = (bf16[1024,512]{1,0:T(8,128)(2,1)S(1)}, f32[1024,512]{1,0:T(8,128)}) fusion(bf16[6144,512]{1,0:T(8,128)(2,1)S(1)} %bitcast.100, s32[6144]{0:T(1024)S(1)} %sub.64, bf16[1024,512]{1,0:T(8,128)(2,1)S(1)} %copy-done.4), kind=kOutput, calls=%fused_computation.97 | convolution fusion | flops 6450315264 | bytes 10510336 | tf_op jit(solution)/shard_map/dot_general | solution.py:212
  199.6 35.8 %share.1 = (bf16[1024,512]{1,0:T(8,128)(2,1)S(1)}, bf16[512,512]{1,0:T(8,128)(2,1)S(1)}) custom-call(bf16[1024,512]{1,0:T(8,128)(2,1)S(1)} %get-tuple-element.20.refs_0_, f32[512,512]{1,0:T(8,128)S(1)} %copy-done.1), custom_call_target="tpu_custom_call" | custom-call | tf_op jit(solution)/shard_map/share/pallas_call | solution.py:141
  235.4 6.4 %conditional.1 = (f32[1024,512]{1,0:T(8,128)}) conditional(s32[]{:T(128)} %convert_element_type.63, () %tuple.11, (f32[1024,512]{1,0:T(8,128)}, f32[512,512]{1,0:T(8,128)S(1)}) %tuple.19), branch_computations={%region_2.3_spmd, %region_3.4_spmd} | conditional | flops 3221225472 | bytes 5242888 | solution.py:216
  235.4 6.4 %fusion.63 = f32[1024,512]{1,0:T(8,128)} fusion(f32[1024,512]{1,0:T(8,128)} %get-tuple-element.12, f32[512,512]{1,0:T(8,128)S(1)} %get-tuple-element.13), kind=kOutput, calls=%fused_computation.98 | convolution fusion | flops 3221225472 | bytes 5242880 | tf_op jit(solution)/shard_map/cond/branch_1_fun/dot_general | solution.py:218
  241.8 4.3 %select_select_fusion = f32[1024,512]{1,0:T(8,128)} fusion(f32[1024,512]{1,0:T(8,128)} %get-tuple-element.21, f32[1024,512]{1,0:T(8,128)} %get-tuple-element.22, bf16[1024,512]{1,0:T(8,128)(2,1)S(1)} %get-tuple-element.16, bf16[512,512]{1,0:T(8,128)(2,1)S(1)} %get-tuple-element.17, pred[1024]{0:T(1024)(128)(4,1)S(1)} %add_compare_fusion, pred[]{:T(512)S(6)} %eq.168), kind=kOutput, calls=%fused_computation.21 | convolution fusion | flops 538443776 | bytes 7865345 | tf_op jit(solution)/shard_map/dot_general | solution.py:221
  (27 shorter events, 1.0 us)
Async XLA Ops:
  6.5 5.0 %copy-start = (bf16[1,512,512]{2,1,0:T(8,128)(2,1)S(1)}, bf16[1,512,512]{2,1,0:T(8,128)(2,1)}, u32[]{:S(2)}) copy-start(bf16[1,512,512]{2,1,0:T(8,128)(2,1)} %param.11) | copy-start | bytes 1572868
  6.5 5.1 %copy-start.3 = (bf16[1,512,256]{2,1,0:T(8,128)(2,1)S(1)}, bf16[1,512,256]{2,1,0:T(8,128)(2,1)}, u32[]{:S(2)}) copy-start(bf16[1,512,256]{2,1,0:T(8,128)(2,1)} %param.12) | copy-start | bytes 786436
  6.5 57.1 %all-gather.3.cloned.1.call-start = ((), (), s32[]{:S(2)}) async-start(), calls=%async_computation.2 | async-start | bytes 4456448 | tf_op jit(solution)/shard_map/all_gather | solution.py:177
  69.7 47.9 %all-to-all-start = ((bf16[16,24,4096]{2,1,0:T(8,128)(2,1)}), bf16[16,24,4096]{2,1,0:T(8,128)(2,1)}, u32[]{:S(2)}, u32[]{:S(2)}) async-start(bf16[16,24,4096]{2,1,0:T(8,128)(2,1)} %bitcast.92), calls=%async_computation | async-start | bytes 6291456 | tf_op jit(solution)/shard_map/all_to_all | solution.py:205
  125.7 4.9 %copy-start.2 = (s32[8,4096]{1,0:T(8,128)S(1)}, s32[8,4096]{1,0:T(8,128)}, u32[]{:S(2)}) copy-start(s32[8,4096]{1,0:T(8,128)} %param.13) | copy-start | bytes 393220
  125.7 60.0 %all-to-all-start.1 = ((bf16[8,16,48,384]{3,2,1,0:T(8,128)(2,1)}), bf16[8,16,48,384]{3,2,1,0:T(8,128)(2,1)}, u32[]{:S(2)}, u32[]{:S(2)}) async-start(bf16[8,16,48,384]{3,2,1,0:T(8,128)(2,1)} %bitcast.89), calls=%async_computation.1 | async-start | bytes 9437184 | tf_op jit(solution)/shard_map/all_to_all | solution.py:209
  185.7 5.9 %copy-start.4 = (bf16[1024,512]{1,0:T(8,128)(2,1)S(1)}, bf16[1024,512]{1,0:T(8,128)(2,1)}, u32[]{:S(2)}) copy-start(bf16[1024,512]{1,0:T(8,128)(2,1)} %param.14) | copy-start | bytes 3145732
  191.6 8.0 %copy-start.1 = (f32[512,512]{1,0:T(8,128)S(1)}, f32[512,512]{1,0:T(8,128)}, u32[]{:S(2)}) copy-start(f32[512,512]{1,0:T(8,128)} %refs_1_.1) | copy-start | bytes 3145732
Sparse Core Ops, SparseCore 0:
  9.5 54.1 all-gather.2

commit v3 on v2

--- a/solution.py
+++ b/solution.py
@@ -158,6 +158,216 @@
     )(asm, pinv)
 
 
+def nt(a, b):
+    return lax.dot_general(a, b, (((1,), (1,)), ((), ())), preferred_element_type=F32)
+
+
+def exchange_kernel(
+    nr, nc, fr, fc, cs, rs,
+    left, child, core, right, maps, xrecv,
+    lbuf, mixing, tri, mask, slots, pick32, pick_cols, pick_rows, zsend, zrecv, xsend,
+    ls, lr, zs, zr, xs, xr,
+):
+    row = lax.axis_index("row")
+    col = lax.axis_index("col")
+    mesh = pl.DeviceIdType.MESH
+    i32 = jnp.int32
+    nb, width = maps.shape[1:]
+    half, quarter = width // 2, width // 4
+    nt_steps = nb // 2
+    y, z = col // 4, lax.rem(col, 4)
+
+    def at(dy, dz):
+        return lax.rem(y + dy + 4, 4) * 4 + lax.rem(z + dz + 4, 4)
+
+    def off(h, p, s):
+        return at(s, p) if h == 0 else at(p, s)
+
+    def piece(h, block, part):
+        size = half if part is None else quarter
+        start = h * half + (0 if part is None else part * quarter)
+        return pl.ds(pl.multiple_of(block * width + start, quarter), size)
+
+    def hop(h, m, src_off, part, to):
+        where = piece(h, off(h, *src_off), part)
+        return pltpu.make_async_remote_copy(
+            lbuf.at[where], lbuf.at[where], ls.at[h, m], lr.at[h, m],
+            device_id={"col": off(h, *to)}, device_id_type=mesh)
+
+    def arrived(h, m, src_off, part):
+        where = piece(h, off(h, *src_off), part)
+        pltpu.make_async_remote_copy(
+            lbuf.at[where], lbuf.at[where], ls.at[h, m], lr.at[h, m],
+            device_id={"col": col}, device_id_type=mesh).wait_recv()
+
+    sent = []
+
+    def go(h, m, src_off, part, to):
+        copy = hop(h, m, src_off, part, to)
+        copy.start()
+        sent.append(copy)
+
+    ks = (0, -1, 1, 2)
+
+    def spread(h, n):
+        go(h, 4 + 4 * n, (ks[n], 0), None, (0, 1))
+        go(h, 5 + 4 * n, (ks[n], 0), None, (0, -1))
+
+    def onward(h, n):
+        arrived(h, 4 + 4 * n, (ks[n], -1), None)
+        go(h, 6 + 4 * n, (ks[n], -1), 0, (0, 1))
+        arrived(h, 5 + 4 * n, (ks[n], 1), None)
+        go(h, 7 + 4 * n, (ks[n], 1), 1, (0, -1))
+
+    def last(h, n):
+        arrived(h, 6 + 4 * n, (ks[n], -2), 0)
+        arrived(h, 7 + 4 * n, (ks[n], 2), 1)
+
+    lbuf[pl.ds(pl.multiple_of(col * width, width), width), :] = left[...]
+    greet(nr, nc, row, col)
+    for h in range(2):
+        go(h, 0, (0, 0), None, (1, 0))
+        go(h, 1, (0, 0), None, (-1, 0))
+    for h in range(2):
+        spread(h, 0)
+
+    mixing[...] = jnp.dot(core[...], right[...], preferred_element_type=F32).astype(BF)
+    before = lax.broadcasted_iota(i32, (width, width), 0) < lax.broadcasted_iota(i32, (width, width), 1)
+    tri[...] = jnp.where(before, 1.0, 0.0).astype(BF)
+
+    for h in range(2):
+        arrived(h, 0, (-1, 0), None)
+        go(h, 2, (-1, 0), 0, (1, 0))
+        arrived(h, 1, (1, 0), None)
+        go(h, 3, (1, 0), 1, (-1, 0))
+    for h in range(2):
+        spread(h, 1)
+        spread(h, 2)
+
+    def ranks(rows):
+        counted = jnp.dot(mask[0:rows, :].astype(BF), tri[...], preferred_element_type=F32)
+        slots[0:rows, :] = jnp.where(mask[0:rows, :] > 0.5, counted, -1.0)
+
+    own = maps[row, pl.ds(col, 1), :] // fc
+    mask[0:nc, :] = jnp.where(own == lax.broadcasted_iota(i32, (nc, width), 0), 1.0, 0.0)
+    ranks(nc)
+    steps_c = lax.broadcasted_iota(i32, (cs, width), 0).astype(F32)
+    for g in range(nc):
+        pick32[g * cs : (g + 1) * cs, :] = jnp.where(slots[g : g + 1, :] == steps_c, 1.0, 0.0)
+    pick_cols[...] = pick32[...].astype(BF)
+
+    for h in range(2):
+        onward(h, 0)
+
+    groups = lax.broadcasted_iota(i32, (nr, width), 0)
+    for b in range(nb):
+        mask[b * nr : (b + 1) * nr, :] = jnp.where(maps[row, b : b + 1, :] // fr == groups, 1.0, 0.0)
+    ranks(nb * nr)
+
+    for h in range(2):
+        arrived(h, 2, (-2, 0), 0)
+        arrived(h, 3, (2, 0), 1)
+        spread(h, 3)
+
+    steps_r = lax.broadcasted_iota(i32, (rs, width), 0).astype(F32)
+
+    def make_rows(b):
+        eight = slots[pl.ds(pl.multiple_of(b * nr, nr), nr), :]
+        for g in range(nr):
+            hit = jnp.where(eight[g : g + 1, :] == steps_r, 1.0, 0.0)
+            pick_rows[b, g * rs : (g + 1) * rs, :] = hit.astype(BF)
+
+    each(0, nb, make_rows)
+
+    for h in range(2):
+        onward(h, 1)
+        onward(h, 2)
+    for h in range(2):
+        onward(h, 3)
+    for n in range(4):
+        for h in range(2):
+            last(h, n)
+
+    def col_copy(t, d, to, whose):
+        return pltpu.make_async_remote_copy(
+            zsend.at[t, to], zrecv.at[t, whose], zs.at[t, d], zr.at[t, d],
+            device_id={"col": to}, device_id_type=mesh)
+
+    def produce(t):
+        rows = pl.ds(pl.multiple_of(t * 2 * width, 2 * width), 2 * width)
+        product = jnp.dot(lbuf[rows, :], mixing[...], preferred_element_type=F32)
+        update = (child[rows, :].astype(F32) - product).astype(BF)
+        picked = nt(pick_cols[...], update).reshape(nc, cs // 8, 8, 2 * width)
+        low = picked[:, :, None, :, :width]
+        high = picked[:, :, None, :, width:]
+        both = jnp.concatenate([low, high], axis=2).reshape(nc, 2 * cs, width)
+        zsend[t] = both.astype(BF)
+        zrecv[t, col] = zsend[t, col]
+        each(1, nc, lambda d: col_copy(t, d, col_peer(col, d), col).start())
+
+    each(0, nt_steps, produce)
+
+    def row_copy(t, d, to, whose):
+        return pltpu.make_async_remote_copy(
+            xsend.at[t, to], xrecv.at[whose, t], xs.at[t, d], xr.at[t, d],
+            device_id={"row": to}, device_id_type=mesh)
+
+    def forward(t):
+        each(1, nc, lambda d: col_copy(t, d, col_from(col, d), col_from(col, d)).wait_recv())
+        got = zrecv[t].astype(F32).reshape(nc, cs // 8, 2, 8, width)
+        for h in range(2):
+            part = got[:, :, h].reshape(nc * cs, width).astype(BF)
+            rows = nt(pick_rows[2 * t + h], part)
+            xsend[t, :, h * rs : (h + 1) * rs, :] = rows.reshape(nr, rs, nc * cs).astype(BF)
+        xrecv[row, t] = xsend[t, row]
+        each(1, nr, lambda d: row_copy(t, d, row_peer(row, d), row).start())
+
+    each(0, nt_steps, forward)
+
+    def finish(t):
+        each(1, nr, lambda d: row_copy(t, d, row_from(row, d), row_from(row, d)).wait_recv())
+        each(1, nr, lambda d: row_copy(t, d, row_peer(row, d), row).wait_send())
+        each(1, nc, lambda d: col_copy(t, d, col_peer(col, d), col).wait_send())
+
+    each(0, nt_steps, finish)
+    for copy in sent:
+        copy.wait_send()
+
+
+def exchange(nr, nc, fr, fc, cs, rs, left, child, core, right, maps):
+    order, width = child.shape
+    rank = left.shape[1]
+    nb = order // width
+    vmem = pl.BlockSpec(memory_space=pltpu.VMEM)
+    dma = pltpu.SemaphoreType.DMA
+    return pl.pallas_call(
+        lambda *refs: exchange_kernel(nr, nc, fr, fc, cs, rs, *refs),
+        out_shape=jax.ShapeDtypeStruct((nr, nb // 2, 2 * rs, nc * cs), BF),
+        in_specs=[vmem] * 5,
+        out_specs=vmem,
+        scratch_shapes=[
+            pltpu.VMEM((order, rank), BF),
+            pltpu.VMEM((rank, width), BF),
+            pltpu.VMEM((width, width), BF),
+            pltpu.VMEM((nb * nr, width), F32),
+            pltpu.VMEM((nb * nr, width), F32),
+            pltpu.VMEM((nc * cs, width), F32),
+            pltpu.VMEM((nc * cs, width), BF),
+            pltpu.VMEM((nb, nr * rs, width), BF),
+            pltpu.VMEM((nb // 2, nc, 2 * cs, width), BF),
+            pltpu.VMEM((nb // 2, nc, 2 * cs, width), BF),
+            pltpu.VMEM((nb // 2, nr, 2 * rs, nc * cs), BF),
+            dma((2, 20)), dma((2, 20)),
+            dma((nb // 2, nc)), dma((nb // 2, nc)),
+            dma((nb // 2, nr)), dma((nb // 2, nr)),
+        ],
+        compiler_params=pltpu.CompilerParams(
+            collective_id=1, has_side_effects=True, vmem_limit_bytes=56 * 1024 * 1024
+        ),
+        name="exchange",
+    )(left, child, core, right, maps)
+
+
 def on_device(
     child_block, left_gen, core_gen, right_gen, child_maps, parent_entries, pivot_inverse
 ):
@@ -174,22 +384,9 @@
     pw = pivot_inverse.shape[0]
     nb = order // width
 
-    left = lax.all_gather(left_gen[0], "col", axis=0, tiled=True)
-    mixing = jnp.dot(core_gen[0], right_gen[0], preferred_element_type=F32).astype(BF)
-
     blocks = child_maps.reshape(nr, nb, width)
     pos = jnp.arange(width, dtype=jnp.int32)
     tri = (pos[:, None] < pos[None, :]).astype(BF)
-    mine = lax.dynamic_index_in_dim(blocks, row_me, 0, keepdims=False)
-    my_cols = lax.dynamic_index_in_dim(mine, col_me, 0, keepdims=False)
-    cmask = (my_cols // fc)[None, :] == jnp.arange(nc, dtype=jnp.int32)[:, None]
-    cslot = block_slots(cmask, tri)
-    pick_cols = (cslot[:, None, :] == jnp.arange(cs, dtype=jnp.int32)[None, :, None]).astype(BF)
-    pick_cols = pick_cols.reshape(nc * cs, width)
-    rmask = (mine // fr)[:, None, :] == jnp.arange(nr, dtype=jnp.int32)[None, :, None]
-    rslot = block_slots(rmask, tri)
-    pick_rows = (rslot[:, :, None, :] == jnp.arange(rs, dtype=jnp.int32)[None, None, :, None]).astype(BF)
-    pick_rows = pick_rows.reshape(nb, nr * rs, width)
     rmask2 = (blocks // fr) == row_me
     rtarget = slot_targets(block_slots(rmask2, tri), blocks - row_me * fr, rs).reshape(nr * nb * rs)
     place_rows = (rtarget[None, :] == jnp.arange(fr, dtype=jnp.int32)[:, None]).astype(BF)
@@ -197,17 +394,9 @@
     ctarget = slot_targets(block_slots(cmask2, tri), blocks - col_me * fc, cs).reshape(nr, nb * cs)
     place_cols = (ctarget[:, :, None] == jnp.arange(fc, dtype=jnp.int32)[None, None, :]).astype(BF)
 
-    product = jnp.dot(left, mixing, preferred_element_type=F32)
-    update = (child_block[0].astype(F32) - product).astype(BF)
-
-    sent = lax.dot_general(pick_cols, update, (((1,), (1,)), ((), ())), preferred_element_type=F32)
-    sent = sent.astype(BF).reshape(nc, cs, order)
-    got = lax.all_to_all(sent, "col", split_axis=0, concat_axis=0, tiled=True)
-    got = got.reshape(nc * cs, nb, width)
-    rows = jnp.einsum("isp,cip->isc", pick_rows, got, preferred_element_type=F32).astype(BF)
-    rows = rows.reshape(nb, nr, rs, nc * cs).transpose(1, 0, 2, 3)
-    moved = lax.all_to_all(rows, "row", split_axis=0, concat_axis=0, tiled=True)
-    moved = moved.reshape(nr, nb * rs, nc * cs)
+    moved = exchange(
+        nr, nc, fr, fc, cs, rs, left_gen[0], child_block[0], core_gen[0], right_gen[0], blocks
+    ).reshape(nr, nb * rs, nc * cs)
     wide = jnp.einsum("nsc,ncf->nsf", moved, place_cols, preferred_element_type=F32).astype(BF)
     placed = jnp.dot(place_rows, wide.reshape(nr * nb * rs, fc), preferred_element_type=F32)
     assembled = parent_entries.astype(F32) + placed

time: 253 us -> 167 us (0.66)
  waiting for transfers between devices: 143 us -> 0 us
  Pallas kernels: 35.8 us -> 134 us
  between operations: 13.6 us -> 0.09 us
  starting transfers between devices: 10.2 us -> 0 us
  local copies, waits for them, and re-layouts: 9.86 us -> 1.8 us
  matrix products: 34.2 us -> 26.8 us
    pallas_call x0 -> x1, Pallas kernels: none -> 99.7 us  [exchange(): pl.pallas_call(lambda *refs: exchange_kernel(nr, nc, fr, fc, cs, rs, *ref...]
    all_to_all x2 -> x0, waiting for transfers between devices: 91 us -> none  [the longest x1 49.8 us: on_device(): moved = lax.all_to_all(rows, 'row', split_axis=0, concat_axis=0, tiled=True)]
    all_gather x1 -> x0, waiting for transfers between devices: 51.8 us -> none  [on_device(): left = lax.all_gather(left_gen[0], 'col', axis=0, tiled=True)]
    all_to_all x2 -> x0, starting transfers between devices: 10.2 us -> none  [the longest x1 5.33 us: on_device(): got = lax.all_to_all(sent, 'col', split_axis=0, concat_axis=0, tiled=True)]
    dot_general x3 -> x0, matrix products: 8.88 us -> none  [the longest x1 5.99 us: on_device(): lax.dot_general(pick_cols, update, (((1,), (1,)), ((), ())), preferred_el...]
    unnamed x13 -> x7, local copies, waits for them, and re-layouts: 6.81 us -> 1.62 us
    reshape x1 -> x0, local copies, waits for them, and re-layouts: 2.69 us -> none  [on_device(): rows = rows.reshape(nb, nr, rs, nc * cs).transpose(1, 0, 2, 3)]
  transfers between devices with their start and end apart: 3 -> 0, of which waited for: 3 -> 0; matrix products, arithmetic and copies ran while one was open for 4% -> 0% of each run, Pallas kernels for 0% -> 0%
where the time goes in v3:
time: 167 us
  Pallas kernels  134 us (80%)
  matrix products  26.8 us (16%)
  other arithmetic  4.55 us (3%)
  local copies, waits for them, and re-layouts  1.8 us (1%)
    pallas_call x1, Pallas kernels, exchange(): pl.pallas_call(lambda *refs: exchange_kernel(nr, nc, fr, fc, cs, rs, *ref...  99.7 us
    pallas_call x1, Pallas kernels, share(): pl.pallas_call(lambda *refs: share_kernel(nr, nc, *refs), out_shape=(jax....  34.1 us
    dot_general x1, matrix products, on_device(): jnp.dot(place_rows, wide.reshape(nr * nb * rs, fc), preferred_element_typ...  8.01 us
    dot_general x1, matrix products, on_device(): jnp.dot(assembled, pivot_inverse, precision=HI, preferred_element_type=F32)  6.37 us
    dot_general x1, matrix products, on_device(): jnp.einsum('nsc,ncf->nsf', moved, place_cols, preferred_element_type=F32)  5.65 us
    reduce_sum x2, other arithmetic, slot_targets(): return jnp.sum(jnp.where(hit, targets[..., None, :] + 1, 0), axis=-1) - 1  4.47 us
    dot_general x1, matrix products, on_device(): jnp.dot(panel_rows, pivot, preferred_element_type=F32)  4.25 us

profile of v3, /device:TPU:0, one launch (start us, length us, event | category | flops | bytes accessed | tf_op | source)
XLA Modules:
  0.0 167.0 jit_solution(10251388340548455151)
XLA Ops:
  0.0 0.0 copy-start.1
  0.0 1.3 fusion.6
  1.3 1.2 fusion.5
  2.5 1.6 copy.26
  4.1 0.0 copy-done.1
  4.1 0.1 subtract_add_fusion.1
  4.2 2.2 %select_reduce_fusion.1 = s32[8,16,24]{2,1,0:T(8,128)S(1)} fusion(s32[8,16,256]{2,1,0:T(8,128)S(1)} %get-tuple-element.19, s32[8,16,256]{2,1,0:T(8,128)S(1)} %fusion.5), kind=kLoop, calls=%fused_computation.9 | loop fusion | flops 2356224 | bytes 274432 | tf_op jit(solution)/shard_map/reduce_sum | solution.py:20
  6.4 2.2 %select_reduce_fusion = s32[8,16,48]{2,1,0:T(8,128)S(1)} fusion(s32[8,16,256]{2,1,0:T(8,128)S(1)} %get-tuple-element.18, s32[8,16,256]{2,1,0:T(8,128)S(1)} %fusion.6), kind=kLoop, calls=%fused_computation.4 | loop fusion | flops 4712448 | bytes 286720 | tf_op jit(solution)/shard_map/reduce_sum | solution.py:20
  8.7 0.1 sub.49
  8.8 0.1 sub.54
  8.9 99.7 %exchange.1 = bf16[8,8,96,384]{3,2,1,0:T(8,128)(2,1)} custom-call(bf16[256,512]{1,0:T(8,128)(2,1)} %bitcast.44, bf16[4096,256]{1,0:T(8,128)(2,1)} %bitcast.37, bf16[512,512]{1,0:T(8,128)(2,1)} %bitcast.43, bf16[512,256]{1,0:T(8,128)(2,1)} %bitcast.45, s32[8,16,256]{2,1,0:T(8,128)} %bitcast.38), custom_call_target="tpu_custom_call" | custom-call | tf_op jit(solution)/shard_map/exchange/pallas_call | solution.py:343
  108.6 0.0 copy-start.2
  108.6 5.6 %fusion.3 = bf16[8,768,512]{2,1,0:T(8,128)(2,1)S(1)} fusion(bf16[8,768,384]{2,1,0:T(8,128)(2,1)} %bitcast.36, s32[8,384]{1,0:T(8,128)S(1)} %sub.54), kind=kOutput, calls=%fused_computation.7 | convolution fusion | flops 2420637696 | bytes 11022336 | tf_op jit(solution)/shard_map/nsc,ncf->nsf/dot_general | solution.py:400
  114.3 0.0 copy-done.2
  114.3 0.0 copy-start
  114.3 8.0 %fusion.42 = (bf16[1024,512]{1,0:T(8,128)(2,1)S(1)}, f32[1024,512]{1,0:T(8,128)}) fusion(bf16[6144,512]{1,0:T(8,128)(2,1)S(1)} %bitcast.46, s32[6144]{0:T(1024)S(1)} %sub.49, bf16[1024,512]{1,0:T(8,128)(2,1)S(1)} %copy-done.2), kind=kOutput, calls=%fused_computation.61 | convolution fusion | flops 6450315264 | bytes 10510336 | tf_op jit(solution)/shard_map/dot_general | solution.py:401
  122.3 0.0 copy-done
  122.3 34.1 %share.1 = (bf16[1024,512]{1,0:T(8,128)(2,1)S(1)}, bf16[512,512]{1,0:T(8,128)(2,1)S(1)}) custom-call(bf16[1024,512]{1,0:T(8,128)(2,1)S(1)} %get-tuple-element.20.refs_0_, f32[512,512]{1,0:T(8,128)S(1)} %copy-done), custom_call_target="tpu_custom_call" | custom-call | tf_op jit(solution)/shard_map/share/pallas_call | solution.py:141
  156.4 6.4 %conditional.1 = (f32[1024,512]{1,0:T(8,128)}) conditional(s32[]{:T(128)} %convert_element_type.27, () %tuple.11, (f32[1024,512]{1,0:T(8,128)}, f32[512,512]{1,0:T(8,128)S(1)}) %tuple.17), branch_computations={%region_2.3_spmd, %region_3.4_spmd} | conditional | flops 3221225472 | bytes 5242888 | solution.py:405
  156.4 6.4 %fusion.43 = f32[1024,512]{1,0:T(8,128)} fusion(f32[1024,512]{1,0:T(8,128)} %get-tuple-element.12, f32[512,512]{1,0:T(8,128)S(1)} %get-tuple-element.13), kind=kOutput, calls=%fused_computation.62 | convolution fusion | flops 3221225472 | bytes 5242880 | tf_op jit(solution)/shard_map/cond/branch_1_fun/dot_general | solution.py:407
  162.8 4.2 %select_select_fusion = f32[1024,512]{1,0:T(8,128)} fusion(f32[1024,512]{1,0:T(8,128)} %get-tuple-element.21, f32[1024,512]{1,0:T(8,128)} %get-tuple-element.22, bf16[1024,512]{1,0:T(8,128)(2,1)S(1)} %get-tuple-element.16, bf16[512,512]{1,0:T(8,128)(2,1)S(1)} %get-tuple-element.17, pred[1024]{0:T(1024)(128)(4,1)S(1)} %add_compare_fusion, pred[]{:T(512)S(6)} %eq.84), kind=kOutput, calls=%fused_computation.11 | convolution fusion | flops 538443776 | bytes 7865345 | tf_op jit(solution)/shard_map/dot_general | solution.py:410
  (3 shorter events, 0.0 us)
Async XLA Ops:
  0.0 4.1 %copy-start.1 = (s32[8,4096]{1,0:T(8,128)S(1)}, s32[8,4096]{1,0:T(8,128)}, u32[]{:S(2)}) copy-start(s32[8,4096]{1,0:T(8,128)} %param.13) | copy-start | bytes 393220
  108.6 5.7 %copy-start.2 = (bf16[1024,512]{1,0:T(8,128)(2,1)S(1)}, bf16[1024,512]{1,0:T(8,128)(2,1)}, u32[]{:S(2)}) copy-start(bf16[1024,512]{1,0:T(8,128)(2,1)} %param.14) | copy-start | bytes 3145732
  114.3 8.0 %copy-start = (f32[512,512]{1,0:T(8,128)S(1)}, f32[512,512]{1,0:T(8,128)}, u32[]{:S(2)}) copy-start(f32[512,512]{1,0:T(8,128)} %refs_1_.1) | copy-start | bytes 3145732

commit v4 on v3

--- a/solution.py
+++ b/solution.py
@@ -61,7 +61,7 @@
     pl.semaphore_wait(barrier, nc + nr - 2)
 
 
-def share_kernel(nr, nc, asm, pinv, panel, pivot, chunk, ss1, rs1, ss2, rs2, ss3, rs3, ss4, rs4):
+def share_kernel(nr, nc, full, pinv, panel, pivot, own_panel, asm, top, chunk, ss1, rs1, ss2, rs2, ss3, rs3, ss4, rs4):
     row = lax.axis_index("row")
     col = lax.axis_index("col")
     mesh = pl.DeviceIdType.MESH
@@ -73,7 +73,7 @@
 
     def pivot_out(d):
         return pltpu.make_async_remote_copy(
-            rows_of(asm, d, vc), rows_of(pivot, d, vc), ss1.at[d], rs1.at[0],
+            rows_of(top, d, vc), rows_of(pivot, d, vc), ss1.at[d], rs1.at[0],
             device_id={"row": d}, device_id_type=mesh)
 
     def panel_out(d):
@@ -97,13 +97,15 @@
 
     @pl.when(col == 0)
     def _():
+        asm[...] = full[...].astype(BF)
         each(1, nc, lambda d: panel_out(d).start())
         chunk[...] = asm[0:pc, :]
 
     @pl.when(row == 0)
     def _():
+        top[...] = full[0 : vc * nr, :].astype(BF)
         each(1, nr, lambda d: pivot_out(d).start())
-        pivot[0:vc, :] = asm[0:vc, :]
+        pivot[0:vc, :] = top[0:vc, :]
 
     @pl.when(row > 0)
     def _():
@@ -118,6 +120,15 @@
     part = jnp.dot(chunk[...].astype(F32), pinv[...], precision=HI, preferred_element_type=F32)
     panel[pl.ds(pl.multiple_of(col * pc, pc), pc), :] = part.astype(BF)
     each(1, nc, lambda d: panel_share(d, col).start())
+
+    @pl.when(col == 0)
+    def _():
+        def rows_panel(i):
+            rows = pl.ds(pl.multiple_of(i * 256, 256), 256)
+            own_panel[rows, :] = jnp.dot(
+                full[rows, :], pinv[...], precision=HI, preferred_element_type=F32)
+
+        each(0, full.shape[0] // 256, rows_panel)
 
     each(1, nr, lambda d: pivot_share(d, row_from(row, d)).wait_recv())
     each(1, nc, lambda d: panel_share(d, col_from(col, d)).wait_recv())
@@ -143,10 +154,13 @@
         out_shape=(
             jax.ShapeDtypeStruct((rows, pw), BF),
             jax.ShapeDtypeStruct((pw, cols), BF),
+            jax.ShapeDtypeStruct((rows, pw), F32),
         ),
         in_specs=[vmem, vmem],
-        out_specs=(vmem, vmem),
+        out_specs=(vmem, vmem, vmem),
         scratch_shapes=[
+            pltpu.VMEM((rows, cols), BF),
+            pltpu.VMEM((pw, cols), BF),
             pltpu.VMEM((rows // nc, pw), BF),
             dma((nr,)), dma((1,)), dma((nc,)), dma((1,)),
             dma((nr,)), dma((nr,)), dma((nc,)), dma((nc,)),
@@ -165,7 +179,7 @@
 def exchange_kernel(
     nr, nc, fr, fc, cs, rs,
     left, child, core, right, maps, xrecv,
-    lbuf, mixing, tri, mask, slots, pick32, pick_cols, pick_rows, zsend, zrecv, xsend,
+    lbuf, msel, product, tri, mask, slots, pick32, pick_cols, pick_rows, zsend, zrecv, xsend,
     ls, lr, zs, zr, xs, xr,
 ):
     row = lax.axis_index("row")
@@ -174,7 +188,7 @@
     i32 = jnp.int32
     nb, width = maps.shape[1:]
     half, quarter = width // 2, width // 4
-    nt_steps = nb // 2
+    steps = nb // 2
     y, z = col // 4, lax.rem(col, 4)
 
     def at(dy, dz):
@@ -223,31 +237,77 @@
         arrived(h, 6 + 4 * n, (ks[n], -2), 0)
         arrived(h, 7 + 4 * n, (ks[n], 2), 1)
 
-    lbuf[pl.ds(pl.multiple_of(col * width, width), width), :] = left[...]
-    greet(nr, nc, row, col)
-    for h in range(2):
-        go(h, 0, (0, 0), None, (1, 0))
-        go(h, 1, (0, 0), None, (-1, 0))
-    for h in range(2):
-        spread(h, 0)
-
-    mixing[...] = jnp.dot(core[...], right[...], preferred_element_type=F32).astype(BF)
-    before = lax.broadcasted_iota(i32, (width, width), 0) < lax.broadcasted_iota(i32, (width, width), 1)
-    tri[...] = jnp.where(before, 1.0, 0.0).astype(BF)
-
-    for h in range(2):
-        arrived(h, 0, (-1, 0), None)
-        go(h, 2, (-1, 0), 0, (1, 0))
-        arrived(h, 1, (1, 0), None)
-        go(h, 3, (1, 0), 1, (-1, 0))
-    for h in range(2):
-        spread(h, 1)
-        spread(h, 2)
+    def pair_of(who, k):
+        kk = k // 2
+        dy = kk + kk // 2 - 2 * (kk // 3)
+        return lax.rem(who // 4 + dy, 4) * 2 + lax.rem(lax.rem(who, 4) // 2 + lax.rem(k, 2), 2)
+
+    def col_copy(k, d, to, whose):
+        t = pair_of(to, k)
+        return pltpu.make_async_remote_copy(
+            zsend.at[t, to], zrecv.at[t, whose], zs.at[k, d], zr.at[k, d],
+            device_id={"col": to}, device_id_type=mesh)
+
+    def mix_copy(d, to, whose):
+        return pltpu.make_async_remote_copy(
+            zsend.at[steps, to], zrecv.at[steps, whose], zs.at[steps, d], zr.at[steps, d],
+            device_id={"col": to}, device_id_type=mesh)
+
+    def issue(k):
+        each(1, nc, lambda d: col_copy(k, d, col_peer(col, d), col).start())
+
+    def pick(t, rows):
+        picked = nt(pick_cols[...], rows).reshape(nc, cs // 8, 8, 2 * width)
+        low = picked[:, :, None, :, :width]
+        high = picked[:, :, None, :, width:]
+        both = jnp.concatenate([low, high], axis=2).reshape(nc, 2 * cs, width)
+        zsend[t] = both.astype(BF)
+        zrecv[t, col] = zsend[t, col]
+
+    def parts(t):
+        got = zrecv[t].astype(F32).reshape(nc, cs // 8, 2, 8, width)
+        return [got[:, :, h].reshape(nc * cs, width) for h in range(2)]
 
     def ranks(rows):
         counted = jnp.dot(mask[0:rows, :].astype(BF), tri[...], preferred_element_type=F32)
         slots[0:rows, :] = jnp.where(mask[0:rows, :] > 0.5, counted, -1.0)
 
+    steps_r = lax.broadcasted_iota(i32, (rs, width), 0).astype(F32)
+
+    def row_copy(k, d, to, whose):
+        t = pair_of(col, k)
+        return pltpu.make_async_remote_copy(
+            xsend.at[t, to], xrecv.at[whose, t], xs.at[k, d], xr.at[k, d],
+            device_id={"row": to}, device_id_type=mesh)
+
+    def forward(k):
+        t = pair_of(col, k)
+        for h in range(2):
+            eight = slots[pl.ds(pl.multiple_of((2 * t + h) * nr, nr), nr), :]
+            for g in range(nr):
+                hit = jnp.where(eight[g : g + 1, :] == steps_r, 1.0, 0.0)
+                pick_rows[h, g * rs : (g + 1) * rs, :] = hit.astype(BF)
+        rows = pl.ds(pl.multiple_of(t * 2 * width, 2 * width), 2 * width)
+        product[...] = nt(msel[...], lbuf[rows, :])
+        each(1, nc, lambda d: col_copy(k, d, col, col_from(col, d)).wait_recv())
+        got = parts(t)
+        for h in range(2):
+            update = (got[h] - product[:, h * width : (h + 1) * width]).astype(BF)
+            chosen = nt(pick_rows[h], update)
+            xsend[t, :, h * rs : (h + 1) * rs, :] = chosen.reshape(nr, rs, nc * cs).astype(BF)
+        xrecv[row, t] = xsend[t, row]
+        each(1, nr, lambda d: row_copy(k, d, row_peer(row, d), row).start())
+
+    lbuf[pl.ds(pl.multiple_of(col * width, width), width), :] = left[...]
+    greet(nr, nc, row, col)
+    for h in range(2):
+        go(h, 0, (0, 0), None, (1, 0))
+        go(h, 1, (0, 0), None, (-1, 0))
+    for h in range(2):
+        spread(h, 0)
+
+    before = lax.broadcasted_iota(i32, (width, width), 0) < lax.broadcasted_iota(i32, (width, width), 1)
+    tri[...] = jnp.where(before, 1.0, 0.0).astype(BF)
     own = maps[row, pl.ds(col, 1), :] // fc
     mask[0:nc, :] = jnp.where(own == lax.broadcasted_iota(i32, (nc, width), 0), 1.0, 0.0)
     ranks(nc)
@@ -255,81 +315,66 @@
     for g in range(nc):
         pick32[g * cs : (g + 1) * cs, :] = jnp.where(slots[g : g + 1, :] == steps_c, 1.0, 0.0)
     pick_cols[...] = pick32[...].astype(BF)
-
+    mixing = jnp.dot(core[...], right[...], preferred_element_type=F32).astype(BF)
+    pick(steps, mixing)
+    each(1, nc, lambda d: mix_copy(d, col_peer(col, d), col).start())
+    each(0, steps, lambda t: pick(
+        t, child[pl.ds(pl.multiple_of(t * 2 * width, 2 * width), 2 * width), :]))
+    issue(0)
+    for h in range(2):
+        arrived(h, 0, (-1, 0), None)
+        go(h, 2, (-1, 0), 0, (1, 0))
+        arrived(h, 1, (1, 0), None)
+        go(h, 3, (1, 0), 1, (-1, 0))
+    for h in range(2):
+        spread(h, 1)
+        spread(h, 2)
     for h in range(2):
         onward(h, 0)
+    issue(1)
 
     groups = lax.broadcasted_iota(i32, (nr, width), 0)
     for b in range(nb):
         mask[b * nr : (b + 1) * nr, :] = jnp.where(maps[row, b : b + 1, :] // fr == groups, 1.0, 0.0)
     ranks(nb * nr)
-
+    each(1, nc, lambda d: mix_copy(d, col, col_from(col, d)).wait_recv())
+    low, high = parts(steps)
+    msel[:, :width] = low.astype(BF)
+    msel[:, width:] = high.astype(BF)
+
+    forward(0)
     for h in range(2):
         arrived(h, 2, (-2, 0), 0)
         arrived(h, 3, (2, 0), 1)
         spread(h, 3)
-
-    steps_r = lax.broadcasted_iota(i32, (rs, width), 0).astype(F32)
-
-    def make_rows(b):
-        eight = slots[pl.ds(pl.multiple_of(b * nr, nr), nr), :]
-        for g in range(nr):
-            hit = jnp.where(eight[g : g + 1, :] == steps_r, 1.0, 0.0)
-            pick_rows[b, g * rs : (g + 1) * rs, :] = hit.astype(BF)
-
-    each(0, nb, make_rows)
-
-    for h in range(2):
+    for h in range(2):
+        last(h, 0)
         onward(h, 1)
         onward(h, 2)
+    issue(2)
+    issue(3)
+    forward(1)
     for h in range(2):
         onward(h, 3)
-    for n in range(4):
-        for h in range(2):
-            last(h, n)
-
-    def col_copy(t, d, to, whose):
-        return pltpu.make_async_remote_copy(
-            zsend.at[t, to], zrecv.at[t, whose], zs.at[t, d], zr.at[t, d],
-            device_id={"col": to}, device_id_type=mesh)
-
-    def produce(t):
-        rows = pl.ds(pl.multiple_of(t * 2 * width, 2 * width), 2 * width)
-        product = jnp.dot(lbuf[rows, :], mixing[...], preferred_element_type=F32)
-        update = (child[rows, :].astype(F32) - product).astype(BF)
-        picked = nt(pick_cols[...], update).reshape(nc, cs // 8, 8, 2 * width)
-        low = picked[:, :, None, :, :width]
-        high = picked[:, :, None, :, width:]
-        both = jnp.concatenate([low, high], axis=2).reshape(nc, 2 * cs, width)
-        zsend[t] = both.astype(BF)
-        zrecv[t, col] = zsend[t, col]
-        each(1, nc, lambda d: col_copy(t, d, col_peer(col, d), col).start())
-
-    each(0, nt_steps, produce)
-
-    def row_copy(t, d, to, whose):
-        return pltpu.make_async_remote_copy(
-            xsend.at[t, to], xrecv.at[whose, t], xs.at[t, d], xr.at[t, d],
-            device_id={"row": to}, device_id_type=mesh)
-
-    def forward(t):
-        each(1, nc, lambda d: col_copy(t, d, col_from(col, d), col_from(col, d)).wait_recv())
-        got = zrecv[t].astype(F32).reshape(nc, cs // 8, 2, 8, width)
-        for h in range(2):
-            part = got[:, :, h].reshape(nc * cs, width).astype(BF)
-            rows = nt(pick_rows[2 * t + h], part)
-            xsend[t, :, h * rs : (h + 1) * rs, :] = rows.reshape(nr, rs, nc * cs).astype(BF)
-        xrecv[row, t] = xsend[t, row]
-        each(1, nr, lambda d: row_copy(t, d, row_peer(row, d), row).start())
-
-    each(0, nt_steps, forward)
-
-    def finish(t):
-        each(1, nr, lambda d: row_copy(t, d, row_from(row, d), row_from(row, d)).wait_recv())
-        each(1, nr, lambda d: row_copy(t, d, row_peer(row, d), row).wait_send())
-        each(1, nc, lambda d: col_copy(t, d, col_peer(col, d), col).wait_send())
-
-    each(0, nt_steps, finish)
+    for h in range(2):
+        last(h, 1)
+        last(h, 2)
+    issue(4)
+    issue(5)
+    forward(2)
+    for h in range(2):
+        last(h, 3)
+    issue(6)
+    issue(7)
+    each(3, steps, forward)
+
+    def finish(k):
+        each(1, nr, lambda d: row_copy(k, d, row, row_from(row, d)).wait_recv())
+        each(1, nr, lambda d: row_copy(k, d, row_peer(row, d), row).wait_send())
+        each(1, nc, lambda d: col_copy(k, d, col_peer(col, d), col).wait_send())
+
+    each(0, steps, finish)
+    each(1, nc, lambda d: mix_copy(d, col_peer(col, d), col).wait_send())
     for copy in sent:
         copy.wait_send()
 
@@ -347,18 +392,19 @@
         out_specs=vmem,
         scratch_shapes=[
             pltpu.VMEM((order, rank), BF),
-            pltpu.VMEM((rank, width), BF),
+            pltpu.VMEM((nc * cs, rank), BF),
+            pltpu.VMEM((nc * cs, 2 * width), F32),
             pltpu.VMEM((width, width), BF),
             pltpu.VMEM((nb * nr, width), F32),
             pltpu.VMEM((nb * nr, width), F32),
             pltpu.VMEM((nc * cs, width), F32),
             pltpu.VMEM((nc * cs, width), BF),
-            pltpu.VMEM((nb, nr * rs, width), BF),
-            pltpu.VMEM((nb // 2, nc, 2 * cs, width), BF),
-            pltpu.VMEM((nb // 2, nc, 2 * cs, width), BF),
+            pltpu.VMEM((2, nr * rs, width), BF),
+            pltpu.VMEM((nb // 2 + 1, nc, 2 * cs, width), BF),
+            pltpu.VMEM((nb // 2 + 1, nc, 2 * cs, width), BF),
             pltpu.VMEM((nb // 2, nr, 2 * rs, nc * cs), BF),
             dma((2, 20)), dma((2, 20)),
-            dma((nb // 2, nc)), dma((nb // 2, nc)),
+            dma((nb // 2 + 1, nc)), dma((nb // 2 + 1, nc)),
             dma((nb // 2, nr)), dma((nb // 2, nr)),
         ],
         compiler_params=pltpu.CompilerParams(
@@ -401,12 +447,7 @@
     placed = jnp.dot(place_rows, wide.reshape(nr * nb * rs, fc), preferred_element_type=F32)
     assembled = parent_entries.astype(F32) + placed
 
-    panel_rows, pivot = share(nr, nc, assembled.astype(BF), pivot_inverse)
-    local_panel = lax.cond(
-        col_me == 0,
-        lambda: jnp.dot(assembled, pivot_inverse, precision=HI, preferred_element_type=F32),
-        lambda: jnp.zeros((fr, pw), F32),
-    )
+    panel_rows, pivot, local_panel = share(nr, nc, assembled, pivot_inverse)
     trailing = assembled - jnp.dot(panel_rows, pivot, preferred_element_type=F32)
     global_rows = row_me * fr + jnp.arange(fr, dtype=jnp.int32)
     lower = jnp.where(col_me == 0, local_panel, trailing)

time: 167 us -> 156 us (0.934)
  matrix products: 26.8 us -> 17 us
  Pallas kernels: 134 us -> 131 us
    dot_general x1 -> x0, matrix products: 6.37 us -> none  [on_device(): jnp.dot(assembled, pivot_inverse, precision=HI, preferred_element_type=F32)]
    pallas_call x1, Pallas kernels: 99.7 us -> 95.3 us  [exchange(): pl.pallas_call(lambda *refs: exchange_kernel(nr, nc, fr, fc, cs, rs, *ref...]
    dot_general x1, matrix products: 4.25 us -> 2.12 us  [on_device(): jnp.dot(panel_rows, pivot, preferred_element_type=F32)]
    pallas_call x1, Pallas kernels: 34.1 us -> 36.1 us  [share(): pl.pallas_call(lambda *refs: share_kernel(nr, nc, *refs), out_shape=(jax....]
where the time goes in v4:
time: 156 us
  Pallas kernels  131 us (84%)
  matrix products  17 us (11%)
  other arithmetic  5.45 us (3%)
  local copies, waits for them, and re-layouts  1.8 us (1%)
    pallas_call x1, Pallas kernels, exchange(): pl.pallas_call(lambda *refs: exchange_kernel(nr, nc, fr, fc, cs, rs, *ref...  95.3 us
    pallas_call x1, Pallas kernels, share(): pl.pallas_call(lambda *refs: share_kernel(nr, nc, *refs), out_shape=(jax....  36.1 us
    dot_general x1, matrix products, on_device(): jnp.dot(place_rows, wide.reshape(nr * nb * rs, fc), preferred_element_typ...  6.66 us
    dot_general x1, matrix products, on_device(): jnp.einsum('nsc,ncf->nsf', moved, place_cols, preferred_element_type=F32)  5.82 us
    reduce_sum x2, other arithmetic, slot_targets(): return jnp.sum(jnp.where(hit, targets[..., None, :] + 1, 0), axis=-1) - 1  4.47 us

profile of v4, /device:TPU:0, one launch (start us, length us, event | category | flops | bytes accessed | tf_op | source)
XLA Modules:
  0.0 155.8 jit_solution(11126319946017224278)
XLA Ops:
  0.0 1.2 fusion.6
  1.2 1.2 fusion.5
  2.5 1.6 %copy.26 = s32[1,8,16,256]{3,2,1,0:T(8,128)} copy(s32[1,8,16,256]{3,1,2,0:T(8,128)} %bitcast.39) | data formatting | bytes 262144
  4.1 1.0 subtract_add_fusion.1
  5.0 2.2 %select_reduce_fusion.1 = s32[8,16,24]{2,1,0:T(8,128)S(1)} fusion(s32[8,16,256]{2,1,0:T(8,128)S(1)} %get-tuple-element.12, s32[8,16,256]{2,1,0:T(8,128)S(1)} %fusion.5), kind=kLoop, calls=%fused_computation.9 | loop fusion | flops 2356224 | bytes 274432 | tf_op jit(solution)/shard_map/reduce_sum | solution.py:20
  7.3 2.2 %select_reduce_fusion = s32[8,16,48]{2,1,0:T(8,128)S(1)} fusion(s32[8,16,256]{2,1,0:T(8,128)S(1)} %get-tuple-element.11, s32[8,16,256]{2,1,0:T(8,128)S(1)} %fusion.6), kind=kLoop, calls=%fused_computation.4 | loop fusion | flops 4712448 | bytes 286720 | tf_op jit(solution)/shard_map/reduce_sum | solution.py:20
  9.5 0.1 sub.49
  9.6 0.1 sub.54
  9.7 95.3 %exchange.1 = bf16[8,8,96,384]{3,2,1,0:T(8,128)(2,1)} custom-call(bf16[256,512]{1,0:T(8,128)(2,1)} %bitcast.42, bf16[4096,256]{1,0:T(8,128)(2,1)} %bitcast.35, bf16[512,512]{1,0:T(8,128)(2,1)} %bitcast.41, bf16[512,256]{1,0:T(8,128)(2,1)} %bitcast.43, s32[8,16,256]{2,1,0:T(8,128)} %bitcast.36), custom_call_target="tpu_custom_call" | custom-call | tf_op jit(solution)/shard_map/exchange/pallas_call | solution.py:388
  105.0 0.0 copy-start.1
  105.1 5.8 %fusion.3 = bf16[8,768,512]{2,1,0:T(8,128)(2,1)S(1)} fusion(bf16[8,768,384]{2,1,0:T(8,128)(2,1)} %bitcast.34, s32[8,384]{1,0:T(8,128)S(1)} %sub.54), kind=kOutput, calls=%fused_computation.7 | convolution fusion | flops 2420637696 | bytes 11022336 | tf_op jit(solution)/shard_map/nsc,ncf->nsf/dot_general | solution.py:446
  110.9 0.0 copy-done.1
  110.9 0.0 copy-start
  110.9 6.7 %convert_add_fusion.refs_0_ = f32[1024,512]{1,0:T(8,128)S(1)} fusion(bf16[1024,512]{1,0:T(8,128)(2,1)S(1)} %copy-done.1, bf16[6144,512]{1,0:T(8,128)(2,1)S(1)} %bitcast.44, s32[6144]{0:T(1024)S(1)} %sub.49), kind=kOutput, calls=%fused_computation.12 | convolution fusion | flops 6449790976 | bytes 9461760 | tf_op jit(solution)/shard_map/dot_general | solution.py:447
  117.6 0.0 copy-done
  117.6 36.1 %share.1 = (bf16[1024,512]{1,0:T(8,128)(2,1)S(1)}, bf16[512,512]{1,0:T(8,128)(2,1)S(1)}, f32[1024,512]{1,0:T(8,128)S(1)}) custom-call(f32[1024,512]{1,0:T(8,128)S(1)} %convert_add_fusion.refs_0_, f32[512,512]{1,0:T(8,128)S(1)} %copy-done), custom_call_target="tpu_custom_call" | custom-call | tf_op jit(solution)/shard_map/share/pallas_call | solution.py:152
  153.7 2.1 %select_select_fusion = f32[1024,512]{1,0:T(8,128)} fusion(f32[1024,512]{1,0:T(8,128)S(1)} %convert_add_fusion.refs_0_, f32[1024,512]{1,0:T(8,128)S(1)} %get-tuple-element.8, bf16[1024,512]{1,0:T(8,128)(2,1)S(1)} %get-tuple-element.9, bf16[512,512]{1,0:T(8,128)(2,1)S(1)} %get-tuple-element.10, pred[1024]{0:T(1024)(128)(4,1)S(1)} %add_compare_fusion, ...), kind=kOutput, calls=%fused_computation.11 | convolution fusion | flops 538443776 | bytes 7865345 | tf_op jit(solution)/shard_map/dot_general | solution.py:451
  (3 shorter events, 0.0 us)
Async XLA Ops:
  105.0 5.8 %copy-start.1 = (bf16[1024,512]{1,0:T(8,128)(2,1)S(1)}, bf16[1024,512]{1,0:T(8,128)(2,1)}, u32[]{:S(2)}) copy-start(bf16[1024,512]{1,0:T(8,128)(2,1)} %param.12) | copy-start | bytes 3145732
  110.9 6.7 %copy-start = (f32[512,512]{1,0:T(8,128)S(1)}, f32[512,512]{1,0:T(8,128)}, u32[]{:S(2)}) copy-start(f32[512,512]{1,0:T(8,128)} %refs_1_.1) | copy-start | bytes 3145732

commit v5 on v4

v5 whole, which is shorter than its diff:
```python
import jax
import jax.numpy as jnp
from jax import lax
from jax.experimental import pallas as pl
from jax.experimental.pallas import tpu as pltpu
from jax.sharding import PartitionSpec as P

BF = jnp.bfloat16
F32 = jnp.float32
HI = lax.Precision.HIGHEST


def col_peer(me, d):
    y = lax.rem(me // 4 + d // 4, 4)
    z = lax.rem(lax.rem(me, 4) + lax.rem(d, 4), 4)
    return y * 4 + z


def row_peer(me, d):
    x = lax.rem(me // 2 + d // 2, 4)
    core = lax.rem(lax.rem(me, 2) + lax.rem(d, 2), 2)
    return x * 2 + core


def col_from(me, d):
    y = lax.rem(me // 4 + 4 - d // 4, 4)
    z = lax.rem(lax.rem(me, 4) + 4 - lax.rem(d, 4), 4)
    return y * 4 + z


def row_from(me, d):
    x = lax.rem(me // 2 + 4 - d // 2, 4)
    core = lax.rem(lax.rem(me, 2) + lax.rem(d, 2), 2)
    return x * 2 + core


def each(low, high, body):
    def step(i, carry):
        body(i)
        return carry

    lax.fori_loop(low, high, step, 0)


def greet(nr, nc, row, col):
    barrier = pltpu.get_barrier_semaphore()
    each(1, nc, lambda d: pl.semaphore_signal(
        barrier, inc=1, device_id={"col": col_peer(col, d)}, device_id_type=pl.DeviceIdType.MESH))
    each(1, nr, lambda d: pl.semaphore_signal(
        barrier, inc=1, device_id={"row": row_peer(row, d)}, device_id_type=pl.DeviceIdType.MESH))
    pl.semaphore_wait(barrier, nc + nr - 2)


def nt(a, b):
    return lax.dot_general(a, b, (((1,), (1,)), ((), ())), preferred_element_type=F32)


def front_kernel(
    nr, nc, fr, fc, cs, rs,
    left, child_in, core, right, maps, parent_in, pinv_in,
    asm, panel, pivot, own_panel,
    child, parent, pinv, lbuf, msel, product, tri, mask, slots, far_slots, digits, sel,
    pick32, pick_cols, pick_rows, row_at, col_at, place_cols, place_rows, wide,
    zsend, zrecv, xsend, xrecv, asm16, top16, chunk,
    ls, lr, zs, zr, xs, xr, ss1, rs1, ss2, rs2, ss3, rs3, ss4, rs4, loads,
):
    row = lax.axis_index("row")
    col = lax.axis_index("col")
    mesh = pl.DeviceIdType.MESH
    i32 = jnp.int32
    width = child.shape[1]
    nb = child.shape[0] // width
    half, quarter = width // 2, width // 4
    steps = nb // 2
    y, z = col // 4, lax.rem(col, 4)

    def at(dy, dz):
        return lax.rem(y + dy + 4, 4) * 4 + lax.rem(z + dz + 4, 4)

    def off(h, p, s):
        return at(s, p) if h == 0 else at(p, s)

    def piece(h, block, part):
        size = half if part is None else quarter
        start = h * half + (0 if part is None else part * quarter)
        return pl.ds(pl.multiple_of(block * width + start, quarter), size)

    def hop(h, m, src_off, part, to):
        where = piece(h, off(h, *src_off), part)
        return pltpu.make_async_remote_copy(
            lbuf.at[where], lbuf.at[where], ls.at[h, m], lr.at[h, m],
            device_id={"col": off(h, *to)}, device_id_type=mesh)

    def arrived(h, m, src_off, part):
        where = piece(h, off(h, *src_off), part)
        pltpu.make_async_remote_copy(
            lbuf.at[where], lbuf.at[where], ls.at[h, m], lr.at[h, m],
            device_id={"col": col}, device_id_type=mesh).wait_recv()

    sent = []

    def go(h, m, src_off, part, to):
        copy = hop(h, m, src_off, part, to)
        copy.start()
        sent.append(copy)

    ks = (0, -1, 1, 2)

    def spread(h, n):
        go(h, 4 + 4 * n, (ks[n], 0), None, (0, 1))
        go(h, 5 + 4 * n, (ks[n], 0), None, (0, -1))

    def onward(h, n):
        arrived(h, 4 + 4 * n, (ks[n], -1), None)
        go(h, 6 + 4 * n, (ks[n], -1), 0, (0, 1))
        arrived(h, 5 + 4 * n, (ks[n], 1), None)
        go(h, 7 + 4 * n, (ks[n], 1), 1, (0, -1))

    def last(h, n):
        arrived(h, 6 + 4 * n, (ks[n], -2), 0)
        arrived(h, 7 + 4 * n, (ks[n], 2), 1)

    def pair_of(who, k):
        kk = k // 2
        dy = kk + kk // 2 - 2 * (kk // 3)
        return lax.rem(who // 4 + dy, 4) * 2 + lax.rem(lax.rem(who, 4) // 2 + lax.rem(k, 2), 2)

    def col_copy(k, d, to, whose):
        t = pair_of(to, k)
        return pltpu.make_async_remote_copy(
            zsend.at[t, to], zrecv.at[t, whose], zs.at[k, d], zr.at[k, d],
            device_id={"col": to}, device_id_type=mesh)

    def mix_copy(d, to, whose):
        return pltpu.make_async_remote_copy(
            zsend.at[steps, to], zrecv.at[steps, whose], zs.at[steps, d], zr.at[steps, d],
            device_id={"col": to}, device_id_type=mesh)

    def issue(k):
        each(1, nc, lambda d: col_copy(k, d, col_peer(col, d), col).start())

    def pick(t, rows):
        picked = nt(pick_cols[...], rows).reshape(nc, cs // 8, 8, 2 * width)
        low = picked[:, :, None, :, :width]
        high = picked[:, :, None, :, width:]
        both = jnp.concatenate([low, high], axis=2).reshape(nc, 2 * cs, width)
        zsend[t] = both.astype(BF)
        zrecv[t, col] = zsend[t, col]

    def parts(t):
        got = zrecv[t].astype(F32).reshape(nc, cs // 8, 2, 8, width)
        return [got[:, :, h].reshape(nc * cs, width) for h in range(2)]

    def ranks(rows, into):
        counted = jnp.dot(mask[0:rows, :].astype(BF), tri[...], preferred_element_type=F32)
        into[0:rows, :] = jnp.where(mask[0:rows, :] > 0.5, counted, -1.0)

    steps_r = lax.broadcasted_iota(i32, (rs, width), 0).astype(F32)

    def row_copy(k, d, to, whose):
        t = pair_of(col, k)
        return pltpu.make_async_remote_copy(
            xsend.at[t, to], xrecv.at[whose, t], xs.at[k, d], xr.at[k, d],
            device_id={"row": to}, device_id_type=mesh)

    def forward(k):
        t = pair_of(col, k)
        for h in range(2):
            eight = slots[pl.ds(pl.multiple_of((2 * t + h) * nr, nr), nr), :]
            for g in range(nr):
                hit = jnp.where(eight[g : g + 1, :] == steps_r, 1.0, 0.0)
                pick_rows[h, g * rs : (g + 1) * rs, :] = hit.astype(BF)
        rows = pl.ds(pl.multiple_of(t * 2 * width, 2 * width), 2 * width)
        product[...] = nt(msel[...], lbuf[rows, :])
        each(1, nc, lambda d: col_copy(k, d, col, col_from(col, d)).wait_recv())
        got = parts(t)
        for h in range(2):
            update = (got[h] - product[:, h * width : (h + 1) * width]).astype(BF)
            chosen = nt(pick_rows[h], update)
            xsend[t, :, h * rs : (h + 1) * rs, :] = chosen.reshape(nr, rs, nc * cs).astype(BF)
        xrecv[row, t] = xsend[t, row]
        each(1, nr, lambda d: row_copy(k, d, row_peer(row, d), row).start())

    def split(targets):
        high = targets // 32
        return high.astype(F32), (targets - high * 32).astype(F32)

    def far_rows():
        for b in range(nb):
            here = maps[:, b * width : (b + 1) * width]
            mask[b * nr : (b + 1) * nr, :] = jnp.where(here // fr == row, 1.0, 0.0)
            high, low = split(here - row * fr + 1)
            digits[b] = jnp.concatenate([high, low], axis=0).astype(BF)
        ranks(nb * nr, far_slots)
        size = nr * rs
        sub = lax.broadcasted_iota(i32, (2 * nr, size), 0)
        lane = lax.broadcasted_iota(i32, (2 * nr, size), 1)
        weight = jnp.where(lane // rs == lax.rem(sub, nr), jnp.where(sub < nr, 32.0, 1.0), 0.0)

        def one(b):
            eight = far_slots[pl.ds(pl.multiple_of(b * nr, nr), nr), :]
            for g in range(nr):
                hit = jnp.where(eight[g : g + 1, :] == steps_r, 1.0, 0.0)
                sel[g * rs : (g + 1) * rs, :] = hit.astype(BF)
            found = nt(digits[b], sel[...]) * weight
            row_at[pl.ds(b, 1), :] = jnp.sum(found, axis=0, keepdims=True) - 1.0

        each(0, nb, one)

    def far_cols():
        size = nc * cs
        sub = lax.broadcasted_iota(i32, (2 * nc, size), 0)
        lane = lax.broadcasted_iota(i32, (2 * nc, size), 1)
        weight = jnp.where(lane // cs == lax.rem(sub, nc), jnp.where(sub < nc, 32.0, 1.0), 0.0)
        spots = lax.broadcasted_iota(i32, (fc, size), 0).astype(F32)

        def one(c):
            for q in range(nc):
                here = maps[pl.ds(c, 1), q * width : (q + 1) * width]
                mask[q : q + 1, :] = jnp.where(here // fc == col, 1.0, 0.0)
                high, low = split(here - col * fc + 1)
                pick32[q : q + 1, :] = high
                pick32[nc + q : nc + q + 1, :] = low
            both = pick32[0 : 2 * nc, :].astype(BF)
            ranks(nc, far_slots)
            for q in range(nc):
                hit = jnp.where(far_slots[q : q + 1, :] == steps_c, 1.0, 0.0)
                pick32[q * cs : (q + 1) * cs, :] = hit
            found = nt(both, pick32[...].astype(BF)) * weight
            col_at[...] = jnp.sum(found, axis=0, keepdims=True) - 1.0
            place_cols[c] = jnp.where(spots == col_at[...], 1.0, 0.0).astype(BF)

        each(0, nr, one)

    def settle(kk):
        for j in range(2):
            each(1, nr, lambda d: row_copy(2 * kk + j, d, row, row_from(row, d)).wait_recv())
        yy = pair_of(col, 2 * kk) // 2

        def widen(c):
            values = xrecv[c, pl.ds(2 * yy, 2)].reshape(4 * rs, nc * cs)
            full = nt(values, place_cols[c]).astype(BF).reshape(4, rs, fc)
            wide[:, pl.ds(pl.multiple_of(c * rs, 16), rs), :] = full

        each(0, nr, widen)
        ahead = lax.broadcasted_iota(i32, (256, nr * rs), 0)

        def rows_of_asm(i):
            rows = pl.ds(pl.multiple_of(i * 256, 256), 256)
            spots = (ahead + i * 256).astype(F32)
            for j in range(4):
                hit = jnp.where(spots == row_at[pl.ds(4 * yy + j, 1), :], 1.0, 0.0)
                place_rows[:, j * nr * rs : (j + 1) * nr * rs] = hit.astype(BF)
            asm[rows, :] += jnp.dot(
                place_rows[...], wide[...].reshape(4 * nr * rs, fc), preferred_element_type=F32)

        each(0, fr // 256, rows_of_asm)

    pc = fr // nc
    vc = pinv.shape[0] // nr

    def rows_of(ref, index, size):
        return ref.at[pl.ds(pl.multiple_of(index * size, size), size)]

    def pivot_out(d):
        return pltpu.make_async_remote_copy(
            rows_of(top16, d, vc), rows_of(pivot, d, vc), ss1.at[d], rs1.at[0],
            device_id={"row": d}, device_id_type=mesh)

    def panel_out(d):
        return pltpu.make_async_remote_copy(
            rows_of(asm16, d, pc), chunk, ss2.at[d], rs2.at[0],
            device_id={"col": d}, device_id_type=mesh)

    def pivot_share(d, whose):
        part = rows_of(pivot, whose, vc)
        return pltpu.make_async_remote_copy(
            part, part, ss3.at[d], rs3.at[d],
            device_id={"row": row_peer(row, d)}, device_id_type=mesh)

    def panel_share(d, whose):
        part = rows_of(panel, whose, pc)
        return pltpu.make_async_remote_copy(
            part, part, ss4.at[d], rs4.at[d],
            device_id={"col": col_peer(col, d)}, device_id_type=mesh)

    def load(i, src, dst):
        return pltpu.make_async_copy(src, dst, loads.at[i])

    load(0, child_in, child).start()
    load(1, parent_in, parent).start()
    load(2, pinv_in, pinv).start()
    lbuf[pl.ds(pl.multiple_of(col * width, width), width), :] = left[...]
    greet(nr, nc, row, col)
    for h in range(2):
        go(h, 0, (0, 0), None, (1, 0))
        go(h, 1, (0, 0), None, (-1, 0))
    for h in range(2):
        spread(h, 0)

    before = lax.broadcasted_iota(i32, (width, width), 0) < lax.broadcasted_iota(i32, (width, width), 1)
    tri[...] = jnp.where(before, 1.0, 0.0).astype(BF)
    own = maps[pl.ds(row, 1), pl.ds(pl.multiple_of(col * width, width), width)] // fc
    mask[0:nc, :] = jnp.where(own == lax.broadcasted_iota(i32, (nc, width), 0), 1.0, 0.0)
    ranks(nc, slots)
    steps_c = lax.broadcasted_iota(i32, (cs, width), 0).astype(F32)
    for g in range(nc):
        pick32[g * cs : (g + 1) * cs, :] = jnp.where(slots[g : g + 1, :] == steps_c, 1.0, 0.0)
    pick_cols[...] = pick32[...].astype(BF)
    mixing = jnp.dot(core[...], right[...], preferred_element_type=F32).astype(BF)
    pick(steps, mixing)
    each(1, nc, lambda d: mix_copy(d, col_peer(col, d), col).start())
    load(0, child_in, child).wait()
    each(0, steps, lambda t: pick(
        t, child[pl.ds(pl.multiple_of(t * 2 * width, 2 * width), 2 * width), :]))
    issue(0)
    for h in range(2):
        arrived(h, 0, (-1, 0), None)
        go(h, 2, (-1, 0), 0, (1, 0))
        arrived(h, 1, (1, 0), None)
        go(h, 3, (1, 0), 1, (-1, 0))
    for h in range(2):
        spread(h, 1)
        spread(h, 2)
    for h in range(2):
        onward(h, 0)
    issue(1)

    groups = lax.broadcasted_iota(i32, (nr, width), 0)
    for b in range(nb):
        there = maps[pl.ds(row, 1), b * width : (b + 1) * width] // fr
        mask[b * nr : (b + 1) * nr, :] = jnp.where(there == groups, 1.0, 0.0)
    ranks(nb * nr, slots)
    each(1, nc, lambda d: mix_copy(d, col, col_from(col, d)).wait_recv())
    low, high = parts(steps)
    msel[:, :width] = low.astype(BF)
    msel[:, width:] = high.astype(BF)

    forward(0)
    for h in range(2):
        arrived(h, 2, (-2, 0), 0)
        arrived(h, 3, (2, 0), 1)
        spread(h, 3)
    for h in range(2):
        last(h, 0)
        onward(h, 1)
        onward(h, 2)
    issue(2)
    issue(3)
    forward(1)
    for h in range(2):
        onward(h, 3)
    for h in range(2):
        last(h, 1)
        last(h, 2)
    issue(4)
    issue(5)
    forward(2)
    for h in range(2):
        last(h, 3)
    issue(6)
    issue(7)
    far_rows()
    forward(3)
    far_cols()
    forward(4)
    load(1, parent_in, parent).wait()
    load(2, pinv_in, pinv).wait()
    asm[...] = parent[...].astype(F32)
    forward(5)
    settle(0)
    forward(6)
    forward(7)
    each(1, 4, settle)

    @pl.when(col == 0)
    def _():
        asm16[...] = asm[...].astype(BF)
        each(1, nc, lambda d: panel_out(d).start())
        chunk[...] = asm16[0:pc, :]

    @pl.when(row == 0)
    def _():
        top16[...] = asm[0 : vc * nr, :].astype(BF)
        each(1, nr, lambda d: pivot_out(d).start())
        pivot[0:vc, :] = top16[0:vc, :]

    @pl.when(row > 0)
    def _():
        pivot_out(row).wait_recv()

    each(1, nr, lambda d: pivot_share(d, row).start())

    @pl.when(col > 0)
    def _():
        panel_out(col).wait_recv()

    part = jnp.dot(chunk[...].astype(F32), pinv[...], precision=HI, preferred_element_type=F32)
    panel[pl.ds(pl.multiple_of(col * pc, pc), pc), :] = part.astype(BF)
    each(1, nc, lambda d: panel_share(d, col).start())

    @pl.when(col == 0)
    def _():
        def rows_panel(i):
            rows = pl.ds(pl.multiple_of(i * 256, 256), 256)
            own_panel[rows, :] = jnp.dot(
                asm[rows, :], pinv[...], precision=HI, preferred_element_type=F32)

        each(0, fr // 256, rows_panel)

    def sent_all(k):
        each(1, nr, lambda d: row_copy(k, d, row_peer(row, d), row).wait_send())
        each(1, nc, lambda d: col_copy(k, d, col_peer(col, d), col).wait_send())

    each(0, steps, sent_all)
    each(1, nc, lambda d: mix_copy(d, col_peer(col, d), col).wait_send())
    for copy in sent:
        copy.wait_send()
    each(1, nr, lambda d: pivot_share(d, row_from(row, d)).wait_recv())
    each(1, nc, lambda d: panel_share(d, col_from(col, d)).wait_recv())
    each(1, nr, lambda d: pivot_share(d, row).wait_send())
    each(1, nc, lambda d: panel_share(d, col).wait_send())

    @pl.when(col == 0)
    def _():
        each(1, nc, lambda d: panel_out(d).wait_send())

    @pl.when(row == 0)
    def _():
        each(1, nr, lambda d: pivot_out(d).wait_send())


def front_parts(nr, nc, cs, rs, left, child, core, right, maps, parent, pinv):
    order, width = child.shape
    rank = left.shape[1]
    fr, fc = parent.shape
    pw = pinv.shape[0]
    nb = order // width
    vmem = pl.BlockSpec(memory_space=pltpu.VMEM)
    anywhere = pl.BlockSpec(memory_space=pl.ANY)
    dma = pltpu.SemaphoreType.DMA
    scratch = pltpu.VMEM
    return pl.pallas_call(
        lambda *refs: front_kernel(nr, nc, fr, fc, cs, rs, *refs),
        out_shape=(
            jax.ShapeDtypeStruct((fr, fc), F32),
            jax.ShapeDtypeStruct((fr, pw), BF),
            jax.ShapeDtypeStruct((pw, fc), BF),
            jax.ShapeDtypeStruct((fr, pw), F32),
        ),
        in_specs=[vmem, anywhere, vmem, vmem, vmem, anywhere, anywhere],
        out_specs=(vmem, vmem, vmem, vmem),
        scratch_shapes=[
            scratch((order, width), BF),
            scratch((fr, fc), BF),
            scratch((pw, pw), F32),
            scratch((order, rank), BF),
            scratch((nc * cs, rank), BF),
            scratch((nc * cs, 2 * width), F32),
            scratch((width, width), BF),
            scratch((nb * nr, width), F32),
            scratch((nb * nr, width), F32),
            scratch((nb * nr, width), F32),
            scratch((nb, 2 * nr, width), BF),
            scratch((nr * rs, width), BF),
            scratch((nc * cs, width), F32),
            scratch((nc * cs, width), BF),
            scratch((2, nr * rs, width), BF),
            scratch((nb, nr * rs), F32),
            scratch((1, nc * cs), F32),
            scratch((nr, fc, nc * cs), BF),
            scratch((256, 4 * nr * rs), BF),
            scratch((4, nr * rs, fc), BF),
            scratch((nb // 2 + 1, nc, 2 * cs, width), BF),
            scratch((nb // 2 + 1, nc, 2 * cs, width), BF),
            scratch((nb // 2, nr, 2 * rs, nc * cs), BF),
            scratch((nr, nb // 2, 2 * rs, nc * cs), BF),
            scratch((fr, fc), BF),
            scratch((pw, fc), BF),
            scratch((fr // nc, fc), BF),
            dma((2, 20)), dma((2, 20)),
            dma((nb // 2 + 1, nc)), dma((nb // 2 + 1, nc)),
            dma((nb // 2, nr)), dma((nb // 2, nr)),
            dma((nr,)), dma((1,)), dma((nc,)), dma((1,)),
            dma((nr,)), dma((nr,)), dma((nc,)), dma((nc,)),
            dma((3,)),
        ],
        compiler_params=pltpu.CompilerParams(
            collective_id=0, has_side_effects=True, vmem_limit_bytes=60 * 1024 * 1024
        ),
        name="front_parts",
    )(left, child, core, right, maps, parent, pinv)


def on_device(
    child_block, left_gen, core_gen, right_gen, child_maps, parent_entries, pivot_inverse
):
    nr = lax.axis_size("row")
    nc = lax.axis_size("col")
    row_me = lax.axis_index("row")
    col_me = lax.axis_index("col")
    order = child_block.shape[1]
    fr, fc = parent_entries.shape
    unit = order // (16 * nr * nr)
    cs = 6 * unit
    rs = 12 * unit
    pw = pivot_inverse.shape[0]
    assembled, panel_rows, pivot, local_panel = front_parts(
        nr, nc, cs, rs, left_gen[0], child_block[0], core_gen[0], right_gen[0], child_maps,
        parent_entries, pivot_inverse,
    )
    trailing = assembled - jnp.dot(panel_rows, pivot, preferred_element_type=F32)
    global_rows = row_me * fr + jnp.arange(fr, dtype=jnp.int32)
    lower = jnp.where(col_me == 0, local_panel, trailing)
    return jnp.where(global_rows[:, None] < pw, assembled, lower)


def solution(mesh):
    return jax.shard_map(
        on_device,
        mesh=mesh,
        in_specs=(
            P("row", None, "col"),
            P("row", "col", None),
            P("row", None, None),
            P("row", None, "col"),
            P(),
            P("row", "col"),
            P(),
        ),
        out_specs=P("row", "col"),
        check_vma=False,
    )
```

time: 156 us -> 138 us (0.88)
  matrix products: 17 us -> 4.75 us
  other arithmetic: 5.45 us -> 0.01 us
  Pallas kernels: 131 us -> 133 us
  local copies, waits for them, and re-layouts: 1.8 us -> 0 us
    dot_general x4 -> x0, matrix products: 14.9 us -> none  [the longest x1 6.66 us: on_device(): jnp.dot(place_rows, wide.reshape(nr * nb * rs, fc), preferred_element_typ...]
    reduce_sum x2 -> x0, other arithmetic: 4.47 us -> none  [slot_targets(): return jnp.sum(jnp.where(hit, targets[..., None, :] + 1, 0), axis=-1) - 1]
    dot_general x1, matrix products: 2.12 us -> 4.75 us  [on_device(): jnp.dot(panel_rows, pivot, preferred_element_type=F32)]
    pallas_call x2 -> x1, Pallas kernels: 131 us -> 133 us  [front_parts(): pl.pallas_call(lambda *refs: front_kernel(nr, nc, fr, fc, cs, rs, *refs),...]
    unnamed x5 -> x0, local copies, waits for them, and re-layouts: 1.62 us -> none
where the time goes in v5:
time: 138 us
  Pallas kernels  133 us (96%)
  matrix products  4.75 us (3%)
    pallas_call x1, Pallas kernels, front_parts(): pl.pallas_call(lambda *refs: front_kernel(nr, nc, fr, fc, cs, rs, *refs),...  133 us
    dot_general x1, matrix products, on_device(): jnp.dot(panel_rows, pivot, preferred_element_type=F32)  4.75 us

profile of v5, /device:TPU:0, one launch (start us, length us, event | category | flops | bytes accessed | tf_op | source)
XLA Modules:
  0.0 138.0 jit_solution(1666926056013468897)
XLA Ops:
  0.0 133.3 %front_parts.1 = (f32[1024,512]{1,0:T(8,128)}, bf16[1024,512]{1,0:T(8,128)(2,1)}, bf16[512,512]{1,0:T(8,128)(2,1)}, f32[1024,512]{1,0:T(8,128)}) custom-call(bf16[256,512]{1,0:T(8,128)(2,1)} %bitcast.8, bf16[4096,256]{1,0:T(8,128)(2,1)} %bitcast.6, bf16[512,512]{1,0:T(8,128)(2,1)} %bitcast.7, bf16[512,256]{1,0:T(8,128)(2,1)} %bitcast.9, s32[8,4096]{1,0:T(8,128)} %refs_4_.1, ...), custom_call_target="tpu_custom_call" | custom-call | tf_op jit(solution)/shard_map/front_parts/pallas_call | solution.py:443
  133.3 4.8 %select_select_fusion = f32[1024,512]{1,0:T(8,128)} fusion(f32[1024,512]{1,0:T(8,128)} %get-tuple-element.9, f32[1024,512]{1,0:T(8,128)} %get-tuple-element.10, bf16[1024,512]{1,0:T(8,128)(2,1)} %get-tuple-element.11, bf16[512,512]{1,0:T(8,128)(2,1)} %get-tuple-element.12, pred[1024]{0:T(1024)(128)(4,1)S(1)} %add_compare_fusion, pred[]{:T(512)S(6)} %eq.3), kind=kOutput, calls=%fused_computation | convolution fusion | flops 538443776 | bytes 7865345 | tf_op jit(solution)/shard_map/dot_general | solution.py:512
  (1 shorter events, 0.0 us)

commit v6 on v5

--- a/solution.py
+++ b/solution.py
@@ -48,7 +48,7 @@
         barrier, inc=1, device_id={"col": col_peer(col, d)}, device_id_type=pl.DeviceIdType.MESH))
     each(1, nr, lambda d: pl.semaphore_signal(
         barrier, inc=1, device_id={"row": row_peer(row, d)}, device_id_type=pl.DeviceIdType.MESH))
-    pl.semaphore_wait(barrier, nc + nr - 2)
+    return lambda: pl.semaphore_wait(barrier, nc + nr - 2)
 
 
 def nt(a, b):
@@ -58,11 +58,12 @@
 def front_kernel(
     nr, nc, fr, fc, cs, rs,
     left, child_in, core, right, maps, parent_in, pinv_in,
-    asm, panel, pivot, own_panel,
+    front,
+    asm, panel, pivot, solved,
     child, parent, pinv, lbuf, msel, product, tri, mask, slots, far_slots, digits, sel,
     pick32, pick_cols, pick_rows, row_at, col_at, place_cols, place_rows, wide,
-    zsend, zrecv, xsend, xrecv, asm16, top16, chunk,
-    ls, lr, zs, zr, xs, xr, ss1, rs1, ss2, rs2, ss3, rs3, ss4, rs4, loads,
+    zsend, zrecv, xsend, xrecv, asm16, top16,
+    ls, lr, zs, zr, xs, xr, ss1, rs1, ss2, rs2, ss3, rs3, ss4, rs4, loads, stores,
 ):
     row = lax.axis_index("row")
     col = lax.axis_index("col")
@@ -267,9 +268,12 @@
             rows_of(top16, d, vc), rows_of(pivot, d, vc), ss1.at[d], rs1.at[0],
             device_id={"row": d}, device_id_type=mesh)
 
-    def panel_out(d):
-        return pltpu.make_async_remote_copy(
-            rows_of(asm16, d, pc), chunk, ss2.at[d], rs2.at[0],
+    def half_of(h, index):
+        return pl.ds(pl.multiple_of(index * pc + h * (pc // 2), pc // 2), pc // 2)
+
+    def panel_out(h, d):
+        return pltpu.make_async_remote_copy(
+            asm16.at[half_of(h, d)], panel.at[half_of(h, d)], ss2.at[h, d], rs2.at[h],
             device_id={"col": d}, device_id_type=mesh)
 
     def pivot_share(d, whose):
@@ -278,11 +282,15 @@
             part, part, ss3.at[d], rs3.at[d],
             device_id={"row": row_peer(row, d)}, device_id_type=mesh)
 
-    def panel_share(d, whose):
-        part = rows_of(panel, whose, pc)
-        return pltpu.make_async_remote_copy(
-            part, part, ss4.at[d], rs4.at[d],
+    def panel_share(h, d, whose):
+        part = panel.at[half_of(h, whose)]
+        return pltpu.make_async_remote_copy(
+            part, part, ss4.at[h, d], rs4.at[h, d],
             device_id={"col": col_peer(col, d)}, device_id_type=mesh)
+
+    def store(i):
+        rows = pl.ds(pl.multiple_of(i * 256, 256), 256)
+        return pltpu.make_async_copy(asm.at[rows], front.at[rows], stores.at[i])
 
     def load(i, src, dst):
         return pltpu.make_async_copy(src, dst, loads.at[i])
@@ -291,13 +299,7 @@
     load(1, parent_in, parent).start()
     load(2, pinv_in, pinv).start()
     lbuf[pl.ds(pl.multiple_of(col * width, width), width), :] = left[...]
-    greet(nr, nc, row, col)
-    for h in range(2):
-        go(h, 0, (0, 0), None, (1, 0))
-        go(h, 1, (0, 0), None, (-1, 0))
-    for h in range(2):
-        spread(h, 0)
-
+    greeted = greet(nr, nc, row, col)
     before = lax.broadcasted_iota(i32, (width, width), 0) < lax.broadcasted_iota(i32, (width, width), 1)
     tri[...] = jnp.where(before, 1.0, 0.0).astype(BF)
     own = maps[pl.ds(row, 1), pl.ds(pl.multiple_of(col * width, width), width)] // fc
@@ -307,13 +309,30 @@
     for g in range(nc):
         pick32[g * cs : (g + 1) * cs, :] = jnp.where(slots[g : g + 1, :] == steps_c, 1.0, 0.0)
     pick_cols[...] = pick32[...].astype(BF)
+    greeted()
+    for h in range(2):
+        go(h, 0, (0, 0), None, (1, 0))
+        go(h, 1, (0, 0), None, (-1, 0))
+    for h in range(2):
+        spread(h, 0)
+
     mixing = jnp.dot(core[...], right[...], preferred_element_type=F32).astype(BF)
     pick(steps, mixing)
     each(1, nc, lambda d: mix_copy(d, col_peer(col, d), col).start())
     load(0, child_in, child).wait()
-    each(0, steps, lambda t: pick(
-        t, child[pl.ds(pl.multiple_of(t * 2 * width, 2 * width), 2 * width), :]))
-    issue(0)
+
+    def pick_and_send(i):
+        t = lax.rem(pair_of(col, 0) + i, steps)
+        pick(t, child[pl.ds(pl.multiple_of(t * 2 * width, 2 * width), 2 * width), :])
+        for j in range(2):
+            ty, tz = t // 2, lax.rem(t, 2) * 2 + j
+            to = ty * 4 + tz
+
+            @pl.when(to != col)
+            def _():
+                col_copy(0, lax.rem(ty - y + 4, 4) * 4 + lax.rem(tz - z + 4, 4), to, col).start()
+
+    each(0, steps, pick_and_send)
     for h in range(2):
         arrived(h, 0, (-1, 0), None)
         go(h, 2, (-1, 0), 0, (1, 0))
@@ -324,7 +343,6 @@
         spread(h, 2)
     for h in range(2):
         onward(h, 0)
-    issue(1)
 
     groups = lax.broadcasted_iota(i32, (nr, width), 0)
     for b in range(nb):
@@ -345,39 +363,42 @@
         last(h, 0)
         onward(h, 1)
         onward(h, 2)
+    issue(1)
     issue(2)
-    issue(3)
     forward(1)
     for h in range(2):
         onward(h, 3)
     for h in range(2):
         last(h, 1)
         last(h, 2)
+    issue(3)
     issue(4)
+    forward(2)
+    for h in range(2):
+        last(h, 3)
     issue(5)
-    forward(2)
-    for h in range(2):
-        last(h, 3)
-    issue(6)
-    issue(7)
     far_rows()
     forward(3)
+    issue(6)
     far_cols()
     forward(4)
+    issue(7)
     load(1, parent_in, parent).wait()
     load(2, pinv_in, pinv).wait()
     asm[...] = parent[...].astype(F32)
     forward(5)
     settle(0)
     forward(6)
+    settle(1)
     forward(7)
-    each(1, 4, settle)
+    each(2, 4, settle)
 
     @pl.when(col == 0)
     def _():
         asm16[...] = asm[...].astype(BF)
-        each(1, nc, lambda d: panel_out(d).start())
-        chunk[...] = asm16[0:pc, :]
+        for h in range(2):
+            each(1, nc, lambda d: panel_out(h, d).start())
+        panel[0:pc, :] = asm16[0:pc, :]
 
     @pl.when(row == 0)
     def _():
@@ -390,23 +411,13 @@
         pivot_out(row).wait_recv()
 
     each(1, nr, lambda d: pivot_share(d, row).start())
-
-    @pl.when(col > 0)
-    def _():
-        panel_out(col).wait_recv()
-
-    part = jnp.dot(chunk[...].astype(F32), pinv[...], precision=HI, preferred_element_type=F32)
-    panel[pl.ds(pl.multiple_of(col * pc, pc), pc), :] = part.astype(BF)
-    each(1, nc, lambda d: panel_share(d, col).start())
-
-    @pl.when(col == 0)
-    def _():
-        def rows_panel(i):
-            rows = pl.ds(pl.multiple_of(i * 256, 256), 256)
-            own_panel[rows, :] = jnp.dot(
-                asm[rows, :], pinv[...], precision=HI, preferred_element_type=F32)
-
-        each(0, fr // 256, rows_panel)
+    for h in range(2):
+
+        @pl.when(col > 0)
+        def _():
+            panel_out(h, col).wait_recv()
+
+        each(1, nc, lambda d: panel_share(h, d, col).start())
 
     def sent_all(k):
         each(1, nr, lambda d: row_copy(k, d, row_peer(row, d), row).wait_send())
@@ -417,17 +428,46 @@
     for copy in sent:
         copy.wait_send()
     each(1, nr, lambda d: pivot_share(d, row_from(row, d)).wait_recv())
-    each(1, nc, lambda d: panel_share(d, col_from(col, d)).wait_recv())
+    solved[...] = jnp.dot(
+        pinv[...], pivot[...].astype(F32), precision=HI, preferred_element_type=F32).astype(BF)
+
+    def close(dy):
+        def arrive(dz):
+            d = dy * 4 + dz
+            for h in range(2):
+                panel_share(h, d, col_from(col, d)).wait_recv()
+
+        each(jnp.where(dy == 0, 1, 0), 4, arrive)
+        i = lax.rem(y + 4 - dy, 4)
+        rows = pl.ds(pl.multiple_of(i * 256, 256), 256)
+        lower = jnp.logical_or(row > 0, i >= vc * nr // 256)
+
+        @pl.when(jnp.logical_and(lower, col > 0))
+        def _():
+            asm[rows, :] -= jnp.dot(panel[rows, :], solved[...], preferred_element_type=F32)
+
+        @pl.when(jnp.logical_and(lower, col == 0))
+        def _():
+            asm[rows, :] = jnp.dot(
+                asm[rows, :], pinv[...], precision=HI, preferred_element_type=F32)
+
+        store(i).start()
+
+    each(0, 4, close)
     each(1, nr, lambda d: pivot_share(d, row).wait_send())
-    each(1, nc, lambda d: panel_share(d, col).wait_send())
+    for h in range(2):
+        each(1, nc, lambda d: panel_share(h, d, col).wait_send())
 
     @pl.when(col == 0)
     def _():
-        each(1, nc, lambda d: panel_out(d).wait_send())
+        for h in range(2):
+            each(1, nc, lambda d: panel_out(h, d).wait_send())
 
     @pl.when(row == 0)
     def _():
         each(1, nr, lambda d: pivot_out(d).wait_send())
+
+    each(0, 4, lambda i: store(i).wait())
 
 
 def front_parts(nr, nc, cs, rs, left, child, core, right, maps, parent, pinv):
@@ -442,15 +482,14 @@
     scratch = pltpu.VMEM
     return pl.pallas_call(
         lambda *refs: front_kernel(nr, nc, fr, fc, cs, rs, *refs),
-        out_shape=(
-            jax.ShapeDtypeStruct((fr, fc), F32),
-            jax.ShapeDtypeStruct((fr, pw), BF),
-            jax.ShapeDtypeStruct((pw, fc), BF),
-            jax.ShapeDtypeStruct((fr, pw), F32),
-        ),
+        out_shape=jax.ShapeDtypeStruct((fr, fc), F32),
         in_specs=[vmem, anywhere, vmem, vmem, vmem, anywhere, anywhere],
-        out_specs=(vmem, vmem, vmem, vmem),
+        out_specs=anywhere,
         scratch_shapes=[
+            scratch((fr, fc), F32),
+            scratch((fr, pw), BF),
+            scratch((pw, fc), BF),
+            scratch((pw, fc), BF),
             scratch((order, width), BF),
             scratch((fr, fc), BF),
             scratch((pw, pw), F32),
@@ -477,13 +516,12 @@
             scratch((nr, nb // 2, 2 * rs, nc * cs), BF),
             scratch((fr, fc), BF),
             scratch((pw, fc), BF),
-            scratch((fr // nc, fc), BF),
             dma((2, 20)), dma((2, 20)),
             dma((nb // 2 + 1, nc)), dma((nb // 2 + 1, nc)),
             dma((nb // 2, nr)), dma((nb // 2, nr)),
-            dma((nr,)), dma((1,)), dma((nc,)), dma((1,)),
-            dma((nr,)), dma((nr,)), dma((nc,)), dma((nc,)),
-            dma((3,)),
+            dma((nr,)), dma((1,)), dma((2, nc)), dma((2,)),
+            dma((nr,)), dma((nr,)), dma((2, nc)), dma((2, nc)),
+            dma((3,)), dma((4,)),
         ],
         compiler_params=pltpu.CompilerParams(
             collective_id=0, has_side_effects=True, vmem_limit_bytes=60 * 1024 * 1024
@@ -497,22 +535,14 @@
 ):
     nr = lax.axis_size("row")
     nc = lax.axis_size("col")
-    row_me = lax.axis_index("row")
-    col_me = lax.axis_index("col")
     order = child_block.shape[1]
-    fr, fc = parent_entries.shape
     unit = order // (16 * nr * nr)
     cs = 6 * unit
     rs = 12 * unit
-    pw = pivot_inverse.shape[0]
-    assembled, panel_rows, pivot, local_panel = front_parts(
+    return front_parts(
         nr, nc, cs, rs, left_gen[0], child_block[0], core_gen[0], right_gen[0], child_maps,
         parent_entries, pivot_inverse,
     )
-    trailing = assembled - jnp.dot(panel_rows, pivot, preferred_element_type=F32)
-    global_rows = row_me * fr + jnp.arange(fr, dtype=jnp.int32)
-    lower = jnp.where(col_me == 0, local_panel, trailing)
-    return jnp.where(global_rows[:, None] < pw, assembled, lower)
 
 
 def solution(mesh):

time: 138 us -> 130 us (0.942)
  Pallas kernels: 133 us -> 127 us
  matrix products: 4.75 us -> 0 us
  local copies, waits for them, and re-layouts: 0 us -> 3.08 us
    pallas_call x1, Pallas kernels: 133 us -> 127 us  [front_parts(): pl.pallas_call(lambda *refs: front_kernel(nr, nc, fr, fc, cs, rs, *refs),...]
    dot_general x1 -> x0, matrix products: 4.75 us -> none  [on_device(): jnp.dot(panel_rows, pivot, preferred_element_type=F32)]
    unnamed x0 -> x1, local copies, waits for them, and re-layouts: none -> 3.08 us
where the time goes in v6:
time: 130 us
  Pallas kernels  127 us (98%)
  local copies, waits for them, and re-layouts  3.08 us (2%)
    pallas_call x1, Pallas kernels, front_parts(): pl.pallas_call(lambda *refs: front_kernel(nr, nc, fr, fc, cs, rs, *refs),...  127 us
    unnamed x1, local copies, waits for them, and re-layouts  3.08 us

profile of v6, /device:TPU:0, one launch (start us, length us, event | category | flops | bytes accessed | tf_op | source)
XLA Modules:
  0.0 129.8 jit_solution(7271018261084882942)
XLA Ops:
  0.0 126.7 %front_parts.1 = f32[1024,512]{1,0:T(8,128)} custom-call(bf16[256,512]{1,0:T(8,128)(2,1)} %bitcast.6, bf16[4096,256]{1,0:T(8,128)(2,1)} %bitcast.4, bf16[512,512]{1,0:T(8,128)(2,1)} %bitcast.5, bf16[512,256]{1,0:T(8,128)(2,1)} %bitcast.7, s32[8,4096]{1,0:T(8,128)} %refs_4_.1, bf16[1024,512]{1,0:T(8,128)(2,1)} %refs_5_.1, f32[512,512]{1,0:T(8,128)} %refs_6_.1), custom_call_target="tpu_custom_call" | custom-call | tf_op jit(solution)/shard_map/front_parts/pallas_call | solution.py:483
  126.7 3.1 %copy.9 = f32[1024,512]{1,0:T(8,128)} copy(f32[1024,512]{1,0:T(8,128)} %front_parts.1) | data formatting | bytes 4194304

commit v7 on v6

--- a/solution.py
+++ b/solution.py
@@ -7,7 +7,6 @@
 
 BF = jnp.bfloat16
 F32 = jnp.float32
-HI = lax.Precision.HIGHEST
 
 
 def col_peer(me, d):
@@ -59,7 +58,7 @@
     nr, nc, fr, fc, cs, rs,
     left, child_in, core, right, maps, parent_in, pinv_in,
     front,
-    asm, panel, pivot, solved,
+    asm, panel, pivot, solved, pin_high, pin_low,
     child, parent, pinv, lbuf, msel, product, tri, mask, slots, far_slots, digits, sel,
     pick32, pick_cols, pick_rows, row_at, col_at, place_cols, place_rows, wide,
     zsend, zrecv, xsend, xrecv, asm16, top16,
@@ -233,10 +232,55 @@
 
         each(0, nr, one)
 
-    def settle(kk):
+    pc = fr // nc
+    vc = pinv.shape[0] // nr
+
+    def rows_of(ref, index, size):
+        return ref.at[pl.ds(pl.multiple_of(index * size, size), size)]
+
+    def pivot_out(d):
+        return pltpu.make_async_remote_copy(
+            rows_of(top16, d, vc), rows_of(pivot, d, vc), ss1.at[d], rs1.at[0],
+            device_id={"row": d}, device_id_type=mesh)
+
+    def half_of(h, index):
+        return pl.ds(pl.multiple_of(index * pc + h * (pc // 2), pc // 2), pc // 2)
+
+    def panel_out(h, d):
+        return pltpu.make_async_remote_copy(
+            asm16.at[half_of(h, d)], panel.at[half_of(h, d)], ss2.at[h, d], rs2.at[h],
+            device_id={"col": d}, device_id_type=mesh)
+
+    def pivot_share(d, whose):
+        part = rows_of(pivot, whose, vc)
+        return pltpu.make_async_remote_copy(
+            part, part, ss3.at[d], rs3.at[d],
+            device_id={"row": row_peer(row, d)}, device_id_type=mesh)
+
+    def panel_share(h, d, whose):
+        part = panel.at[half_of(h, whose)]
+        return pltpu.make_async_remote_copy(
+            part, part, ss4.at[h, d], rs4.at[h, d],
+            device_id={"col": col_peer(col, d)}, device_id_type=mesh)
+
+    def store(i):
+        rows = pl.ds(pl.multiple_of(i * 256, 256), 256)
+        return pltpu.make_async_copy(asm.at[rows], front.at[rows], stores.at[i])
+
+    def settle(kk, last):
+        yy = pair_of(col, 2 * kk) // 2
+        ahead = lax.broadcasted_iota(i32, (256, nr * rs), 0)
+
+        def spots_of(i):
+            rows = pl.ds(pl.multiple_of(i * 256, 256), 256)
+            spots = (ahead + i * 256).astype(F32)
+            for j in range(4):
+                hit = jnp.where(spots == row_at[pl.ds(4 * yy + j, 1), :], 1.0, 0.0)
+                place_rows[rows, j * nr * rs : (j + 1) * nr * rs] = hit.astype(BF)
+
+        each(0, fr // 256, spots_of)
         for j in range(2):
             each(1, nr, lambda d: row_copy(2 * kk + j, d, row, row_from(row, d)).wait_recv())
-        yy = pair_of(col, 2 * kk) // 2
 
         def widen(c):
             values = xrecv[c, pl.ds(2 * yy, 2)].reshape(4 * rs, nc * cs)
@@ -244,53 +288,29 @@
             wide[:, pl.ds(pl.multiple_of(c * rs, 16), rs), :] = full
 
         each(0, nr, widen)
-        ahead = lax.broadcasted_iota(i32, (256, nr * rs), 0)
 
         def rows_of_asm(i):
             rows = pl.ds(pl.multiple_of(i * 256, 256), 256)
-            spots = (ahead + i * 256).astype(F32)
-            for j in range(4):
-                hit = jnp.where(spots == row_at[pl.ds(4 * yy + j, 1), :], 1.0, 0.0)
-                place_rows[:, j * nr * rs : (j + 1) * nr * rs] = hit.astype(BF)
             asm[rows, :] += jnp.dot(
-                place_rows[...], wide[...].reshape(4 * nr * rs, fc), preferred_element_type=F32)
+                place_rows[rows, :], wide[...].reshape(4 * nr * rs, fc), preferred_element_type=F32)
+            if last:
+                scatter(i, rows)
 
         each(0, fr // 256, rows_of_asm)
 
-    pc = fr // nc
-    vc = pinv.shape[0] // nr
-
-    def rows_of(ref, index, size):
-        return ref.at[pl.ds(pl.multiple_of(index * size, size), size)]
-
-    def pivot_out(d):
-        return pltpu.make_async_remote_copy(
-            rows_of(top16, d, vc), rows_of(pivot, d, vc), ss1.at[d], rs1.at[0],
-            device_id={"row": d}, device_id_type=mesh)
-
-    def half_of(h, index):
-        return pl.ds(pl.multiple_of(index * pc + h * (pc // 2), pc // 2), pc // 2)
-
-    def panel_out(h, d):
-        return pltpu.make_async_remote_copy(
-            asm16.at[half_of(h, d)], panel.at[half_of(h, d)], ss2.at[h, d], rs2.at[h],
-            device_id={"col": d}, device_id_type=mesh)
-
-    def pivot_share(d, whose):
-        part = rows_of(pivot, whose, vc)
-        return pltpu.make_async_remote_copy(
-            part, part, ss3.at[d], rs3.at[d],
-            device_id={"row": row_peer(row, d)}, device_id_type=mesh)
-
-    def panel_share(h, d, whose):
-        part = panel.at[half_of(h, whose)]
-        return pltpu.make_async_remote_copy(
-            part, part, ss4.at[h, d], rs4.at[h, d],
-            device_id={"col": col_peer(col, d)}, device_id_type=mesh)
-
-    def store(i):
-        rows = pl.ds(pl.multiple_of(i * 256, 256), 256)
-        return pltpu.make_async_copy(asm.at[rows], front.at[rows], stores.at[i])
+    def scatter(i, rows):
+        first = jnp.where(i == 0, 1, 0)
+
+        @pl.when(col == 0)
+        def _():
+            asm16[rows, :] = asm[rows, :].astype(BF)
+            for h in range(2):
+                each(first, 256 // pc, lambda j: panel_out(h, i * (256 // pc) + j).start())
+
+        @pl.when(jnp.logical_and(row == 0, i < vc * nr // 256))
+        def _():
+            top16[rows, :] = asm[rows, :].astype(BF)
+            each(first, 256 // vc, lambda j: pivot_out(i * (256 // vc) + j).start())
 
     def load(i, src, dst):
         return pltpu.make_async_copy(src, dst, loads.at[i])
@@ -354,6 +374,7 @@
     msel[:, :width] = low.astype(BF)
     msel[:, width:] = high.astype(BF)
 
+    issue(1)
     forward(0)
     for h in range(2):
         arrived(h, 2, (-2, 0), 0)
@@ -363,7 +384,6 @@
         last(h, 0)
         onward(h, 1)
         onward(h, 2)
-    issue(1)
     issue(2)
     forward(1)
     for h in range(2):
@@ -385,25 +405,23 @@
     issue(7)
     load(1, parent_in, parent).wait()
     load(2, pinv_in, pinv).wait()
+    pin_high[...] = pinv[...].astype(BF)
+    pin_low[...] = (pinv[...] - pin_high[...].astype(F32)).astype(BF)
     asm[...] = parent[...].astype(F32)
     forward(5)
-    settle(0)
+    settle(0, False)
     forward(6)
-    settle(1)
+    settle(1, False)
     forward(7)
-    each(2, 4, settle)
+    settle(2, False)
+    settle(3, True)
 
     @pl.when(col == 0)
     def _():
-        asm16[...] = asm[...].astype(BF)
-        for h in range(2):
-            each(1, nc, lambda d: panel_out(h, d).start())
         panel[0:pc, :] = asm16[0:pc, :]
 
     @pl.when(row == 0)
     def _():
-        top16[...] = asm[0 : vc * nr, :].astype(BF)
-        each(1, nr, lambda d: pivot_out(d).start())
         pivot[0:vc, :] = top16[0:vc, :]
 
     @pl.when(row > 0)
@@ -428,8 +446,9 @@
     for copy in sent:
         copy.wait_send()
     each(1, nr, lambda d: pivot_share(d, row_from(row, d)).wait_recv())
-    solved[...] = jnp.dot(
-        pinv[...], pivot[...].astype(F32), precision=HI, preferred_element_type=F32).astype(BF)
+    solved[...] = (
+        jnp.dot(pin_high[...], pivot[...], preferred_element_type=F32)
+        + jnp.dot(pin_low[...], pivot[...], preferred_element_type=F32)).astype(BF)
 
     def close(dy):
         def arrive(dz):
@@ -437,19 +456,23 @@
             for h in range(2):
                 panel_share(h, d, col_from(col, d)).wait_recv()
 
-        each(jnp.where(dy == 0, 1, 0), 4, arrive)
         i = lax.rem(y + 4 - dy, 4)
         rows = pl.ds(pl.multiple_of(i * 256, 256), 256)
         lower = jnp.logical_or(row > 0, i >= vc * nr // 256)
 
+        @pl.when(jnp.logical_and(lower, col == 0))
+        def _():
+            high = asm[rows, :].astype(BF)
+            low = (asm[rows, :] - high.astype(F32)).astype(BF)
+            asm[rows, :] = jnp.dot(high, pin_high[...], preferred_element_type=F32) + (
+                jnp.dot(high, pin_low[...], preferred_element_type=F32)
+                + jnp.dot(low, pin_high[...], preferred_element_type=F32))
+
+        each(jnp.where(dy == 0, 1, 0), 4, arrive)
+
         @pl.when(jnp.logical_and(lower, col > 0))
         def _():
             asm[rows, :] -= jnp.dot(panel[rows, :], solved[...], preferred_element_type=F32)
-
-        @pl.when(jnp.logical_and(lower, col == 0))
-        def _():
-            asm[rows, :] = jnp.dot(
-                asm[rows, :], pinv[...], precision=HI, preferred_element_type=F32)
 
         store(i).start()
 
@@ -490,6 +513,8 @@
             scratch((fr, pw), BF),
             scratch((pw, fc), BF),
             scratch((pw, fc), BF),
+            scratch((pw, pw), BF),
+            scratch((pw, pw), BF),
             scratch((order, width), BF),
             scratch((fr, fc), BF),
             scratch((pw, pw), F32),
@@ -508,7 +533,7 @@
             scratch((nb, nr * rs), F32),
             scratch((1, nc * cs), F32),
             scratch((nr, fc, nc * cs), BF),
-            scratch((256, 4 * nr * rs), BF),
+            scratch((fr, 4 * nr * rs), BF),
             scratch((4, nr * rs, fc), BF),
             scratch((nb // 2 + 1, nc, 2 * cs, width), BF),
             scratch((nb // 2 + 1, nc, 2 * cs, width), BF),

time: 130 us -> 128 us (0.985)
  Pallas kernels: 127 us -> 125 us
    pallas_call x1, Pallas kernels: 127 us -> 125 us  [front_parts(): pl.pallas_call(lambda *refs: front_kernel(nr, nc, fr, fc, cs, rs, *refs),...]
where the time goes in v7:
time: 128 us
  Pallas kernels  125 us (98%)
  local copies, waits for them, and re-layouts  3.08 us (2%)
    pallas_call x1, Pallas kernels, front_parts(): pl.pallas_call(lambda *refs: front_kernel(nr, nc, fr, fc, cs, rs, *refs),...  125 us
    unnamed x1, local copies, waits for them, and re-layouts  3.08 us

profile of v7, /device:TPU:0, one launch (start us, length us, event | category | flops | bytes accessed | tf_op | source)
XLA Modules:
  0.0 128.2 jit_solution(10768853065492936752)
XLA Ops:
  0.0 125.1 %front_parts.1 = f32[1024,512]{1,0:T(8,128)} custom-call(bf16[256,512]{1,0:T(8,128)(2,1)} %bitcast.6, bf16[4096,256]{1,0:T(8,128)(2,1)} %bitcast.4, bf16[512,512]{1,0:T(8,128)(2,1)} %bitcast.5, bf16[512,256]{1,0:T(8,128)(2,1)} %bitcast.7, s32[8,4096]{1,0:T(8,128)} %refs_4_.1, bf16[1024,512]{1,0:T(8,128)(2,1)} %refs_5_.1, f32[512,512]{1,0:T(8,128)} %refs_6_.1), custom_call_target="tpu_custom_call" | custom-call | tf_op jit(solution)/shard_map/front_parts/pallas_call | solution.py:506
  125.1 3.1 %copy.9 = f32[1024,512]{1,0:T(8,128)} copy(f32[1024,512]{1,0:T(8,128)} %front_parts.1) | data formatting | bytes 4194304
